TPU v7x, 512 devices: a whole 4x8x8 slice. The times are simulated.
512 devices in a mesh: gx: 32 (over x_lo, y, core), gy: 16 (over z, x_hi).
Axes of the slice: x: 4 (x_hi: 2, x_lo: 2; x = x_hi * 2 + x_lo), y: 8, z: 8, core: 2. Of those that a mesh axis runs over, the one named last changes fastest.
Arguments:
- charges: float32 [2, 786432], P(None, ('gx', 'gy')), may hold values from -6 to 6
- source_slot: int32 [786432], P(('gx', 'gy')), may hold values from 0 to 2047, as said below
- tile_anchor: int32 [8192, 3], P(('gx', 'gy')), may hold values from 0 to 511, as said below
- projection: bfloat16 [8192, 256, 128], P(('gx', 'gy')), may hold values from -0.5 to 0.5
- near_pairs: int32 [4096, 2], P(('gx', 'gy')), may hold values from 0 to 15
- near_blocks: bfloat16 [4096, 2, 128, 128], P(('gx', 'gy')), may hold values from -0.5 to 0.5
- green_real: float32 [512, 512, 32], P(None, 'gx', 'gy'), may hold values from -2 to 4
- green_imag: float32 [512, 512, 32], P(None, 'gx', 'gy'), may hold values from -12 to 12
Outputs:
- potential: float32 [2, 786432], P(None, ('gx', 'gy'))
Inputs may be any that keep to these rules, and one draw needn't show every extreme that they name: `source_slot`: on each device the 1536 sources occupy distinct slots among the device's 16 tiles of 128 slots; the other slots are empty. `tile_anchor`: tile t belongs to device t // 16, devices in the order gx then gy; its anchor's first two coordinates lie in that device's block of 16 x 32 cells, the third between 0 and 28.
All inputs are finite; a program needn't handle non-finite values.
Results may differ from a plain program's by a relative error of at most 0.0036.
Values may be sent and summed in bfloat16 or wider, within the bound.
No kernel may reach another device: no remote copies, remote signals or barrier semaphores. Data moves between devices by JAX's collectives and lax.ppermute only.
A program may use at most 128 MiB of HBM per device.

v0:
```python
import functools

import jax
import jax.numpy as jnp
import ml_dtypes
import numpy as np
from jax import lax
from jax.experimental import pallas as pl
from jax.experimental.pallas import tpu as pltpu
from jax.sharding import PartitionSpec as P

TILES = 16
SLOTS = 128
SOURCES = 1536
NU = 12
UPAD = 16
NV = 40
CELLS = 512
F32 = jnp.float32
BF16 = jnp.bfloat16
VMEM_LIMIT = 48 * 1024 * 1024


def split_table(table):
    high = table.astype(np.float32).astype(ml_dtypes.bfloat16)
    low = (table - high.astype(np.float64)).astype(np.float32).astype(ml_dtypes.bfloat16)
    return high, low


def as_real(theta, inverse):
    sign = -1.0 if inverse else 1.0
    cos, sin = np.cos(theta), sign * np.sin(theta)
    return np.stack([np.stack([cos, sin], -1), np.stack([-sin, cos], -1)], -2)


def z_tables():
    kz = np.arange(32)
    theta = 2.0 * np.pi * (np.outer(kz, kz) % 32) / 32
    forward = as_real(theta, False).reshape(16, 2, 32, 2, 2)
    table = np.einsum("jqzoc,hg->jhqogcz", forward, np.eye(2)).reshape(128, 128)
    backward = as_real(theta, True).reshape(16, 2, 32, 2, 2) / 32.0
    table_back = np.einsum("jqzoc,hg->jhqcgoz", backward, np.eye(2)).reshape(128, 128)
    return table, table_back


def y_tables():
    k = np.arange(16)
    theta = 2.0 * np.pi * (np.outer(k, k) % 16) / 16
    forward = as_real(theta, False)
    both = np.stack([forward, np.stack([forward[:, :, 1], -forward[:, :, 0]], 2)], 0)
    eyes = np.einsum("hg,qr->hgqr", np.eye(2), np.eye(2))
    table = np.einsum("nkjoc,hgqr->jhqcngokr", both, eyes).reshape(128, 256)
    backward = as_real(theta, True) / 512.0
    table_back = np.einsum("kjoc,hgqr->jgrohckq", backward, eyes).reshape(128, 128)
    phi = 2.0 * np.pi * np.outer(np.arange(NV) - 4, k) / 512
    wide = np.broadcast_to(phi[:, None, None, :, None], (NV, 2, 2, 16, 2)).reshape(NV, 128)
    turn = np.stack([np.cos(wide), np.sin(wide)]).astype(np.float32)
    psi = 2.0 * np.pi * (np.outer(np.arange(32), np.arange(NV) - 4) % 32) / 32
    rows = np.concatenate([np.cos(psi), np.sin(psi)], 1)
    rows_back = np.concatenate([np.cos(psi.T), -np.sin(psi.T)], 1)
    return table, table_back, turn, rows, rows_back


def x_tables():
    kx = np.arange(256)
    place = (8 * np.arange(32)[:, None] + np.arange(UPAD)[None, :] - 2).reshape(-1)
    real = np.broadcast_to((np.arange(UPAD) < NU)[None, :], (32, UPAD)).reshape(-1)
    theta = 2.0 * np.pi * (np.outer(kx, place) % 256) / 256
    cos, sin = np.cos(theta) * real, np.sin(theta) * real
    rows = np.concatenate([cos, sin], 0)
    rows_back = np.concatenate([cos.T, -sin.T], 1) / 512.0
    phi = 2.0 * np.pi * kx[:, None] * np.array([0.0, 1.0])[None, :] / 512
    wide = np.repeat(phi, 64, axis=1)
    turn = np.stack([np.cos(wide), np.sin(wide)]).astype(np.float32)
    return rows, rows_back, turn


def spread_table():
    p = np.arange(256)
    lane = (p // 32 % 2) * 128 + (p // 64) * NV + p // 4 % 8
    return (lane[:, None] == np.arange(256)[None, :]).astype(ml_dtypes.bfloat16)


def mm(a, b):
    return lax.dot_general(a, b, (((1,), (0,)), ((), ())), preferred_element_type=F32)


def mm_nt(a, b):
    return lax.dot_general(a, b, (((1,), (1,)), ((), ())), preferred_element_type=F32)


def halves(value):
    high = value.astype(BF16)
    return high, (value - high.astype(F32)).astype(BF16)


def iota(shape, axis):
    return lax.broadcasted_iota(jnp.int32, shape, axis)


def turned(value):
    bit = (iota(value.shape, 1) // 32) % 2
    return jnp.where(bit == 0, pltpu.roll(value, 96, 1), -pltpu.roll(value, 32, 1))


def crossed(value):
    half = iota(value.shape, 1) // 64
    return pltpu.roll(value, 64, 1) + jnp.where(half == 0, value, -value)


def z_places(anchor_ref, shape, axis):
    at = iota(shape, axis)
    tile = (at // 8) % TILES
    z = at % 4
    for t in range(TILES):
        z = z + jnp.where(tile == t, anchor_ref[t, 2], 0)
    return z


def layer_picks(anchor_ref):
    shape = (128, 256)
    z = z_places(anchor_ref, shape, 1)
    row, col = iota(shape, 0), iota(shape, 1)
    want = (col // 128) * 64 + ((col // 4) % 2) * 32 + z
    return jnp.where(row == want, 1.0, 0.0).astype(BF16)


def place(anchor_ref, t):
    x = (anchor_ref[t, 0] & 15) + 1
    y = (anchor_ref[t, 1] & 31) + 1
    starts = (((x + 1) >> 1) * NV + y, (x >> 1) * NV + y)
    return x & 1, starts


def spread_kernel(
    charges_ref, slot_ref, anchor_ref, proj_ref, tab_ref, spread_ref, out_ref, slots_ref, nodes, patch, cells
):
    slot = slot_ref[...]
    pick = jnp.where(iota((SLOTS, SOURCES), 0) == (slot & 127), 1.0, 0.0).astype(BF16)
    row = iota((128, SOURCES), 0)
    charge = jnp.where(row % 8 < 4, charges_ref[0:1, :], charges_ref[1:2, :])
    held = jnp.where(row // 8 == (slot >> 7), charge, 0.0).astype(BF16)
    slots_ref[...] = mm_nt(held, pick)
    for t in range(TILES):
        mine = slots_ref[8 * t : 8 * t + 8, :].astype(BF16)
        nodes[8 * t : 8 * t + 8, :] = mm_nt(mine, proj_ref[t])
    layer = iota((128, 256), 1) % 4 == iota((128, 256), 0) % 4
    high, low = halves(jnp.where(layer, nodes[...], 0.0))
    patch[...] = mm(high, spread_ref[...]) + mm(low, spread_ref[...])
    cells[...] = jnp.zeros_like(cells)
    empty = jnp.zeros((8, 128), F32)
    for t in range(TILES):
        odd, starts = place(anchor_ref, t)
        even_part = patch[8 * t : 8 * t + 8, 0:128]
        odd_part = patch[8 * t : 8 * t + 8, 128:256]
        parts = (jnp.where(odd == 1, odd_part, even_part), jnp.where(odd == 1, even_part, odd_part))
        for h in range(2):
            wide = jnp.concatenate([parts[h], empty], axis=1)
            wide = pltpu.roll(wide, starts[h] & 127, 1)
            lane = pl.multiple_of((starts[h] >> 7) * 128, 128)
            cells[128 * h + 8 * t : 128 * h + 8 * t + 8, pl.ds(lane, 256)] = wide
    picks = layer_picks(anchor_ref)
    phase_high = mm(tab_ref[0], picks).astype(BF16)
    phase_low = mm(tab_ref[1], picks).astype(BF16)
    high, low = halves(cells[...])
    out = mm(phase_high, high) + mm(phase_high, low) + mm(phase_low, high)
    out_ref[...] = out.astype(BF16)


def near_kernel(pairs_ref, slots_ref, blocks_ref, near_ref):
    near_ref[...] = jnp.zeros_like(near_ref)
    row = iota((8, 128), 0)
    for q in range(8):
        source = slots_ref[pl.ds(pl.multiple_of(pairs_ref[q, 1] * 8, 8), 8), :]
        other = pltpu.roll(source, 4, 0)
        plain = jnp.where(row % 4 == 0, source, 0.0).astype(BF16)
        turn = jnp.where(row == 0, -other, jnp.where(row == 4, other, 0.0)).astype(BF16)
        value = mm_nt(plain, blocks_ref[q, 0]) + mm_nt(turn, blocks_ref[q, 1])
        target = pl.ds(pl.multiple_of(pairs_ref[q, 0] * 8, 8), 8)
        near_ref[target, :] = near_ref[target, :] + value


def y_kernel(in_ref, tab_ref, turn_ref, rows_ref, out_ref, hold):
    data = in_ref[...].astype(F32).T.astype(BF16)
    both = mm(data, tab_ref[0]) + mm(data, tab_ref[1])
    cos, sin = turn_ref[0], turn_ref[1]
    hold[...] = jnp.zeros_like(hold)
    for u in range(NU):
        plain = both[NV * u : NV * (u + 1), 0:128]
        turn = both[NV * u : NV * (u + 1), 128:256]
        lines = jnp.concatenate([plain * cos + turn * sin, turn * cos - plain * sin], axis=0)
        high, low = halves(lines)
        out = mm(rows_ref[0], high) + mm(rows_ref[0], low) + mm(rows_ref[1], high)
        hold[pl.ds(u, 32, stride=UPAD), :] = out
    out_ref[...] = hold[...].astype(BF16)


def x_kernel(in_ref, real_ref, imag_ref, rows_ref, back_ref, turn_ref, out_ref):
    data = in_ref[...]
    both = mm(rows_ref[0], data) + mm(rows_ref[1], data)
    cos, sin = turn_ref[0], turn_ref[1]
    value = both[0:256] + turned(both[256:512])
    value = value * cos + turned(value) * sin
    value = crossed(value)

    def wide(green):
        first, second = green[:, 0:256], green[:, 256:512]
        return jnp.concatenate([first, first, second, second], axis=0).T

    value = value * wide(real_ref[...]) - turned(value) * wide(imag_ref[...])
    value = crossed(value)
    value = value * cos - turned(value) * sin
    high, low = halves(jnp.concatenate([value, turned(value)], axis=0))
    out = mm(back_ref[0], high) + mm(back_ref[0], low) + mm(back_ref[1], high)
    out_ref[...] = out.astype(BF16)


def y_back_kernel(in_ref, tab_ref, turn_ref, rows_ref, out_ref, hold, hold_turned):
    data = in_ref[...].astype(F32)
    hold[...] = data
    hold_turned[...] = turned(data)
    cos, sin = turn_ref[0], turn_ref[1]
    lines = []
    for u in range(NU):
        plain = hold[pl.ds(u, 32, stride=UPAD), :]
        turn = hold_turned[pl.ds(u, 32, stride=UPAD), :]
        four = jnp.concatenate(
            [jnp.concatenate([plain, turn], axis=1), jnp.concatenate([turn, -plain], axis=1)], axis=0
        ).astype(BF16)
        both = mm(rows_ref[0], four) + mm(rows_ref[1], four)
        lines.append(both[:, 0:128] * cos - both[:, 128:256] * sin)
    lines.append(jnp.zeros((CELLS - NU * NV, 128), F32))
    high, low = halves(jnp.concatenate(lines, axis=0))
    out = mm_nt(tab_ref[0], high) + mm_nt(tab_ref[0], low) + mm_nt(tab_ref[1], high)
    out_ref[...] = out.astype(BF16)


def gather_kernel(
    in_ref, slot_ref, anchor_ref, proj_ref, near_ref, tab_ref, spread_ref, out_ref, cells, patch, total
):
    picks = layer_picks(anchor_ref)
    phase_high = mm(tab_ref[0], picks).T.astype(BF16)
    phase_low = mm(tab_ref[1], picks).T.astype(BF16)
    data = in_ref[...]
    field = mm(phase_high, data) + mm(phase_low, data)
    cells[...] = field.astype(BF16).astype(F32)
    for t in range(TILES):
        odd, starts = place(anchor_ref, t)
        parts = []
        for h in range(2):
            lane = pl.multiple_of((starts[h] >> 7) * 128, 128)
            wide = cells[128 * h + 8 * t : 128 * h + 8 * t + 8, pl.ds(lane, 256)]
            parts.append(pltpu.roll(wide, (256 - (starts[h] & 127)) & 255, 1)[:, 0:128])
        patch[8 * t : 8 * t + 8, 0:128] = jnp.where(odd == 1, parts[1], parts[0])
        patch[8 * t : 8 * t + 8, 128:256] = jnp.where(odd == 1, parts[0], parts[1])
    layer = iota((128, 256), 1) % 4 == iota((128, 256), 0) % 4
    patch[...] = jnp.where(layer, mm_nt(patch[...].astype(BF16), spread_ref[...]), 0.0)
    for t in range(TILES):
        mine = patch[8 * t : 8 * t + 8, :].astype(BF16)
        total[8 * t : 8 * t + 8, :] = mm(mine, proj_ref[t])
    high, low = halves(total[...] + near_ref[...])
    slot = slot_ref[...]
    pick = jnp.where(iota((SLOTS, SOURCES), 0) == (slot & 127), 1.0, 0.0).astype(BF16)
    value = mm(high, pick) + mm(low, pick)
    tile = iota((128, SOURCES), 0) // 8
    value = jnp.where(tile == (slot >> 7), value, 0.0).reshape(TILES, 8, SOURCES).sum(axis=0)
    out_ref[...] = jnp.concatenate(
        [value[0:4].sum(axis=0, keepdims=True), value[4:8].sum(axis=0, keepdims=True)], axis=0
    )


VM = pl.BlockSpec(memory_space=pltpu.VMEM)
SM = pl.BlockSpec(memory_space=pltpu.SMEM)


def call(kernel, outs, in_specs, scratch, flops, moved):
    return pl.pallas_call(
        kernel,
        out_shape=outs,
        in_specs=in_specs,
        out_specs=[VM] * len(outs),
        scratch_shapes=scratch,
        compiler_params=pltpu.CompilerParams(vmem_limit_bytes=VMEM_LIMIT),
        cost_estimate=pl.CostEstimate(flops=flops, bytes_accessed=moved, transcendentals=0),
    )


def shape(*dims, dtype=F32):
    return jax.ShapeDtypeStruct(dims, dtype)


def swap(cells, axis, rows):
    parts = lax.axis_size(axis)
    moved = lax.all_to_all(cells.reshape(parts, rows, -1), axis, 0, 0, tiled=True)
    return moved.reshape(parts * rows, -1)


def pair(table):
    return jnp.asarray(np.stack(split_table(table)))


def body(charges, source_slot, tile_anchor, projection, near_pairs, near_blocks, green_real, green_imag):
    z_tab, z_back = z_tables()
    y_tab, y_back, y_turn, y_rows, y_rows_back = y_tables()
    x_rows, x_back, x_turn = x_tables()
    spread = jnp.asarray(spread_table())
    slot = source_slot.reshape(1, SOURCES)

    cells, slots = call(
        spread_kernel,
        [shape(128, CELLS, dtype=BF16), shape(128, SLOTS)],
        [VM, VM, SM, VM, VM, VM],
        [pltpu.VMEM((128, 256), F32), pltpu.VMEM((128, 256), F32), pltpu.VMEM((256, CELLS), F32)],
        10**9,
        2 * 10**6,
    )(charges, slot, tile_anchor, projection, pair(z_tab), spread)

    lines = swap(cells, "gy", 8)
    near = call(near_kernel, [shape(128, SLOTS)], [SM, VM, VM], [], 10**8, 10**6)(near_pairs, slots, near_blocks)[0]
    lines = call(
        y_kernel,
        [shape(512, 128, dtype=BF16)],
        [VM] * 4,
        [pltpu.VMEM((512, 128), F32)],
        10**8,
        10**6,
    )(lines, pair(y_tab), jnp.asarray(y_turn), pair(y_rows))[0]
    lines = swap(lines, "gx", UPAD)
    lines = call(x_kernel, [shape(512, 128, dtype=BF16)], [VM] * 6, [], 10**9, 2 * 10**6)(
        lines,
        green_real.transpose(1, 2, 0).reshape(32, 512),
        green_imag.transpose(1, 2, 0).reshape(32, 512),
        pair(x_rows),
        pair(x_back),
        jnp.asarray(x_turn),
    )[0]
    lines = swap(lines, "gx", UPAD)
    cells = call(
        y_back_kernel,
        [shape(128, CELLS, dtype=BF16)],
        [VM] * 4,
        [pltpu.VMEM((512, 128), F32)] * 2,
        10**8,
        10**6,
    )(lines, pair(y_back), jnp.asarray(y_turn), pair(y_rows_back))[0]
    cells = swap(cells, "gy", 8)
    return call(
        gather_kernel,
        [shape(2, SOURCES)],
        [VM, VM, SM, VM, VM, VM, VM],
        [pltpu.VMEM((256, CELLS), F32), pltpu.VMEM((128, 256), F32), pltpu.VMEM((128, SLOTS), F32)],
        10**9,
        2 * 10**6,
    )(cells, slot, tile_anchor, projection, near, pair(z_back), spread)[0]


def solution(mesh):
    return jax.shard_map(
        body,
        mesh=mesh,
        in_specs=(
            P(None, ("gx", "gy")),
            P(("gx", "gy")),
            P(("gx", "gy"), None),
            P(("gx", "gy"), None, None),
            P(("gx", "gy"), None),
            P(("gx", "gy"), None, None, None),
            P(None, "gx", "gy"),
            P(None, "gx", "gy"),
        ),
        out_specs=P(None, ("gx", "gy")),
        check_vma=False,
    )
```

profile of v0, /device:TPU:1, one launch (start us, length us, event | category | flops | bytes accessed | tf_op | source)
XLA Modules:
  0.0 82.5 jit_solution(10563100635155768342)
XLA Ops:
  0.0 0.0 copy-start.18
  0.0 0.8 copy.20.anchor_ref
  0.8 0.0 copy-done.18
  0.8 0.0 copy-done.8
  0.8 0.0 copy-start.6
  0.8 1.2 %copy-done.6 = bf16[16,256,128]{2,1,0:T(8,128)(2,1)S(1)} copy-done((bf16[16,256,128]{2,1,0:T(8,128)(2,1)S(1)}, bf16[16,256,128]{2,1,0:T(8,128)(2,1)}, u32[]{:S(2)}) %copy-start.6) | copy-done | bytes 1048600
  2.0 0.9 %copy-done.12 = bf16[256,256]{1,0:T(8,128)(2,1)S(1)} copy-done((bf16[256,256]{1,0:T(8,128)(2,1)S(1)}, bf16[256,256]{1,0:T(8,128)(2,1)}, u32[]{:S(2)}) %copy-start.12) | copy-done | bytes 131096
  2.9 0.8 %copy-done.15 = bf16[2,128,128]{2,1,0:T(8,128)(2,1)S(1)} copy-done((bf16[2,128,128]{2,1,0:T(8,128)(2,1)S(1)}, bf16[2,128,128]{2,1,0:T(8,128)(2,1)}, u32[]{:S(2)}) %copy-start.15) | copy-done | bytes 65560
  3.8 2.0 %shard_map.181 = (bf16[128,512]{1,0:T(8,128)(2,1)S(1)}, f32[128,128]{1,0:T(8,128)S(1)}) custom-call(f32[2,1536]{1,0:T(2,128)S(1)} %copy-done.8, s32[1,1536]{1,0:T(1,128)S(1)} %reshape.33.slot_ref, s32[16,3]{1,0:T(8,128)S(1)} %copy.20.anchor_ref, bf16[16,256,128]{2,1,0:T(8,128)(2,1)S(1)} %copy-done.6, bf16[2,128,128]{2,1,0:T(8,128)(2,1)S(1)} %copy-done.15, ...), custom_call_target="tpu_custom_call" | custom-call | flops 1000000000 | bytes 2000000 | tf_op jit(solution)/shard_map/pallas_call | solution.py:309
  5.8 0.0 copy-start.1
  5.9 0.0 copy-start.2
  5.9 0.0 copy-start.5
  5.9 23.3 %all_to_all.20 = bf16[16,8,512]{2,1,0:T(8,128)(2,1)S(1)} all-to-all(bf16[16,8,512]{2,1,0:T(8,128)(2,1)S(1)} %bitcast.15), channel_id=1, replica_groups=mesh['gx'=32,'gy'=16] {'gy'}, dimensions={0} | all-to-all | bytes 262144 | tf_op jit(solution)/shard_map/all_to_all | solution.py:294
  29.2 0.0 copy-done.1
  29.2 0.0 copy-done.2
  29.2 0.0 copy-done.5
  29.2 0.0 copy-start.16
  29.2 1.4 %shard_map.182 = bf16[512,128]{1,0:T(8,128)(2,1)} custom-call(bf16[128,512]{1,0:T(8,128)(2,1)S(1)} %bitcast.11, bf16[2,128,256]{2,1,0:T(8,128)(2,1)S(1)} %copy-done.2, f32[2,40,128]{2,1,0:T(8,128)S(1)} %copy-done.1, bf16[2,32,80]{2,1,0:T(8,128)(2,1)S(1)} %copy-done.5), custom_call_target="tpu_custom_call" | custom-call | flops 100000000 | bytes 1000000 | tf_op jit(solution)/shard_map/pallas_call | solution.py:320
  30.7 9.5 %all-to-all-start.1 = ((bf16[32,16,128]{2,1,0:T(8,128)(2,1)}), bf16[32,16,128]{2,1,0:T(8,128)(2,1)S(1)}, u32[]{:S(2)}, u32[]{:S(2)}) async-start(bf16[32,16,128]{2,1,0:T(8,128)(2,1)} %bitcast.2), calls=%async_computation.1 | async-start | bytes 262144 | tf_op jit(solution)/shard_map/all_to_all | solution.py:294
  40.2 0.0 copy-done.16
  40.2 0.0 copy-start.17
  40.3 0.8 copy-done.17
  41.1 8.2 %all-to-all-done.1 = bf16[32,16,128]{2,1,0:T(8,128)(2,1)S(1)} async-done(((bf16[32,16,128]{2,1,0:T(8,128)(2,1)}), bf16[32,16,128]{2,1,0:T(8,128)(2,1)S(1)}, u32[]{:S(2)}, u32[]{:S(2)}) %all-to-all-start.1) | async-done | bytes 131104 | tf_op jit(solution)/shard_map/all_to_all | solution.py:294
  49.3 0.0 copy-done.9
  49.3 0.0 copy-done.10
  49.3 0.0 copy-done.11
  49.3 0.0 copy-start.3
  49.3 0.0 copy-start.4
  49.3 0.0 copy-start.19
  49.3 0.0 copy-start.13
  49.3 0.0 copy-start.14
  49.4 2.0 %shard_map.183 = bf16[512,128]{1,0:T(8,128)(2,1)S(1)} custom-call(bf16[512,128]{1,0:T(8,128)(2,1)S(1)} %bitcast.13, f32[32,512]{1,0:T(8,128)S(1)} %reshape.38.real_ref, f32[32,512]{1,0:T(8,128)S(1)} %reshape.39.imag_ref, bf16[2,512,512]{2,1,0:T(8,128)(2,1)S(1)} %copy-done.9, bf16[2,512,512]{2,1,0:T(8,128)(2,1)S(1)} %copy-done.10, f32[2,256,128]{2,1,0:T(8,128)S(1)} %copy-done.11), custom_call_target="tpu_custom_call" | custom-call | flops 1000000000 | bytes 2000000 | tf_op jit(solution)/shard_map/pallas_call | solution.py:329
  51.3 0.0 copy-start
  51.4 0.0 copy-start.7
  51.4 13.5 %all_to_all.21 = bf16[32,16,128]{2,1,0:T(8,128)(2,1)S(1)} all-to-all(bf16[32,16,128]{2,1,0:T(8,128)(2,1)S(1)} %bitcast.14), channel_id=1, replica_groups=mesh['gx'=32,'gy'=16] {'gx'}, dimensions={0} | all-to-all | bytes 262144 | tf_op jit(solution)/shard_map/all_to_all | solution.py:294
  64.9 0.0 copy-done.3
  64.9 0.0 copy-done.4
  64.9 1.3 %shard_map.184 = bf16[128,512]{1,0:T(8,128)(2,1)} custom-call(bf16[512,128]{1,0:T(8,128)(2,1)S(1)} %bitcast.10, bf16[2,128,128]{2,1,0:T(8,128)(2,1)S(1)} %copy-done.3, f32[2,40,128]{2,1,0:T(8,128)S(1)} %copy-done.1, bf16[2,40,64]{2,1,0:T(8,128)(2,1)S(1)} %copy-done.4), custom_call_target="tpu_custom_call" | custom-call | flops 100000000 | bytes 1000000 | tf_op jit(solution)/shard_map/pallas_call | solution.py:338
  66.2 3.5 %all-to-all-start.3 = ((bf16[16,8,512]{2,1,0:T(8,128)(2,1)}), bf16[16,8,512]{2,1,0:T(8,128)(2,1)S(1)}, u32[]{:S(2)}, u32[]{:S(2)}) async-start(bf16[16,8,512]{2,1,0:T(8,128)(2,1)} %bitcast.8), calls=%async_computation.3 | async-start | bytes 262144 | tf_op jit(solution)/shard_map/all_to_all | solution.py:294
  69.8 0.0 copy-done.19
  69.8 0.1 copy.21.pairs_ref
  69.9 0.0 copy-done
  69.9 1.0 %shard_map.185.near_ref = f32[128,128]{1,0:T(8,128)S(1)} custom-call(s32[8,2]{1,0:T(8,128)S(1)} %copy.21.pairs_ref, f32[128,128]{1,0:T(8,128)S(1)} %get-tuple-element.8.slots_ref, bf16[8,2,128,128]{3,2,1,0:T(8,128)(2,1)S(1)} %copy-done), custom_call_target="tpu_custom_call" | custom-call | flops 100000000 | bytes 1000000 | tf_op jit(solution)/shard_map/pallas_call | solution.py:319
  70.8 9.1 %all-to-all-done.3 = bf16[16,8,512]{2,1,0:T(8,128)(2,1)S(1)} async-done(((bf16[16,8,512]{2,1,0:T(8,128)(2,1)}), bf16[16,8,512]{2,1,0:T(8,128)(2,1)S(1)}, u32[]{:S(2)}, u32[]{:S(2)}) %all-to-all-start.3) | async-done | bytes 131104 | tf_op jit(solution)/shard_map/all_to_all | solution.py:294
  79.9 0.0 copy-done.13
  79.9 0.0 copy-done.14
  79.9 0.0 copy-done.7
  79.9 2.6 %shard_map.186 = f32[2,1536]{1,0:T(2,128)} custom-call(bf16[128,512]{1,0:T(8,128)(2,1)S(1)} %bitcast.12, s32[1,1536]{1,0:T(1,128)S(1)} %reshape.33.slot_ref, s32[16,3]{1,0:T(8,128)S(1)} %copy.20.anchor_ref, bf16[16,256,128]{2,1,0:T(8,128)(2,1)S(1)} %copy-done.7, f32[128,128]{1,0:T(8,128)S(1)} %shard_map.185.near_ref, bf16[2,128,128]{2,1,0:T(8,128)(2,1)S(1)} %copy-done.14, ...), custom_call_target="tpu_custom_call" | custom-call | flops 1000000000 | bytes 2000000 | tf_op jit(solution)/shard_map/pallas_call | solution.py:347
  (9 shorter events, 0.1 us)
Async XLA Ops:
  0.0 0.8 copy-start.18
  0.0 0.8 copy-start.8
  0.8 1.2 %copy-start.6 = (bf16[16,256,128]{2,1,0:T(8,128)(2,1)S(1)}, bf16[16,256,128]{2,1,0:T(8,128)(2,1)}, u32[]{:S(2)}) copy-start(bf16[16,256,128]{2,1,0:T(8,128)(2,1)} %proj_ref.3) | copy-start | bytes 3145732
  2.0 0.9 %copy-start.12 = (bf16[256,256]{1,0:T(8,128)(2,1)S(1)}, bf16[256,256]{1,0:T(8,128)(2,1)}, u32[]{:S(2)}) copy-start(bf16[256,256]{1,0:T(8,128)(2,1)} %constant.22.clone.spread_ref) | copy-start | bytes 393220
  2.9 0.8 %copy-start.15 = (bf16[2,128,128]{2,1,0:T(8,128)(2,1)S(1)}, bf16[2,128,128]{2,1,0:T(8,128)(2,1)}, u32[]{:S(2)}) copy-start(bf16[2,128,128]{2,1,0:T(8,128)(2,1)} %constant.23.clone.tab_ref) | copy-start | bytes 196612
  3.8 45.5 %copy-start.9 = (bf16[2,512,512]{2,1,0:T(8,128)(2,1)S(1)}, bf16[2,512,512]{2,1,0:T(8,128)(2,1)}, u32[]{:S(2)}) copy-start(bf16[2,512,512]{2,1,0:T(8,128)(2,1)} %constant.27.clone.rows_ref) | copy-start | bytes 3145732
  3.8 45.5 %copy-start.10 = (bf16[2,512,512]{2,1,0:T(8,128)(2,1)S(1)}, bf16[2,512,512]{2,1,0:T(8,128)(2,1)}, u32[]{:S(2)}) copy-start(bf16[2,512,512]{2,1,0:T(8,128)(2,1)} %constant.28.clone.back_ref) | copy-start | bytes 3145732
  5.8 23.4 %copy-start.1 = (f32[2,40,128]{2,1,0:T(8,128)S(1)}, f32[2,40,128]{2,1,0:T(8,128)}, u32[]{:S(2)}) copy-start(f32[2,40,128]{2,1,0:T(8,128)} %constant.25.clone.turn_ref) | copy-start | bytes 122884
  5.9 23.4 %copy-start.2 = (bf16[2,128,256]{2,1,0:T(8,128)(2,1)S(1)}, bf16[2,128,256]{2,1,0:T(8,128)(2,1)}, u32[]{:S(2)}) copy-start(bf16[2,128,256]{2,1,0:T(8,128)(2,1)} %constant.24.clone.tab_ref) | copy-start | bytes 393220
  5.9 23.4 %copy-start.5 = (bf16[2,32,80]{2,1,0:T(8,128)(2,1)S(1)}, bf16[2,32,80]{2,1,0:T(8,128)(2,1)}, u32[]{:S(2)}) copy-start(bf16[2,32,80]{2,1,0:T(8,128)(2,1)} %constant.26.clone.rows_ref) | copy-start | bytes 30724
  29.2 11.0 %copy-start.16 = (f32[512,16,2]{0,2,1:T(2,128)S(1)}, f32[512,16,2]{0,2,1:T(2,128)}, u32[]{:S(2)}) copy-start(f32[512,16,2]{0,2,1:T(2,128)} %param.25) | copy-start | bytes 196612
  30.7 18.6 %copy-start.11 = (f32[2,256,128]{2,1,0:T(8,128)S(1)}, f32[2,256,128]{2,1,0:T(8,128)}, u32[]{:S(2)}) copy-start(f32[2,256,128]{2,1,0:T(8,128)} %constant.29.clone.turn_ref) | copy-start | bytes 786436
  30.7 18.6 %all-to-all-start.1 = ((bf16[32,16,128]{2,1,0:T(8,128)(2,1)}), bf16[32,16,128]{2,1,0:T(8,128)(2,1)S(1)}, u32[]{:S(2)}, u32[]{:S(2)}) async-start(bf16[32,16,128]{2,1,0:T(8,128)(2,1)} %bitcast.2), calls=%async_computation.1 | async-start | bytes 262144 | tf_op jit(solution)/shard_map/all_to_all | solution.py:294
  40.2 0.8 %copy-start.17 = (f32[512,16,2]{0,2,1:T(2,128)S(1)}, f32[512,16,2]{0,2,1:T(2,128)}, u32[]{:S(2)}) copy-start(f32[512,16,2]{0,2,1:T(2,128)} %param.26) | copy-start | bytes 196612
  49.3 15.6 %copy-start.3 = (bf16[2,128,128]{2,1,0:T(8,128)(2,1)S(1)}, bf16[2,128,128]{2,1,0:T(8,128)(2,1)}, u32[]{:S(2)}) copy-start(bf16[2,128,128]{2,1,0:T(8,128)(2,1)} %constant.30.clone.tab_ref) | copy-start | bytes 196612
  49.3 15.6 %copy-start.4 = (bf16[2,40,64]{2,1,0:T(8,128)(2,1)S(1)}, bf16[2,40,64]{2,1,0:T(8,128)(2,1)}, u32[]{:S(2)}) copy-start(bf16[2,40,64]{2,1,0:T(8,128)(2,1)} %constant.31.clone.rows_ref) | copy-start | bytes 30724
  49.3 20.4 %copy-start.19 = (s32[8,2]{0,1:T(2,128)S(1)}, s32[8,2]{0,1:T(2,128)}, u32[]{:S(2)}) copy-start(s32[8,2]{0,1:T(2,128)} %param.23) | copy-start | bytes 196
  49.3 30.6 %copy-start.13 = (bf16[256,256]{1,0:T(8,128)(2,1)S(1)}, bf16[256,256]{1,0:T(8,128)(2,1)}, u32[]{:S(2)}) copy-start(bf16[256,256]{1,0:T(8,128)(2,1)} %constant.22.clone.spread_ref) | copy-start | bytes 393220
  49.3 30.6 %copy-start.14 = (bf16[2,128,128]{2,1,0:T(8,128)(2,1)S(1)}, bf16[2,128,128]{2,1,0:T(8,128)(2,1)}, u32[]{:S(2)}) copy-start(bf16[2,128,128]{2,1,0:T(8,128)(2,1)} %constant.32.clone.tab_ref) | copy-start | bytes 196612
  51.3 18.5 %copy-start = (bf16[8,2,128,128]{3,2,1,0:T(8,128)(2,1)S(1)}, bf16[8,2,128,128]{3,2,1,0:T(8,128)(2,1)}, u32[]{:S(2)}) copy-start(bf16[8,2,128,128]{3,2,1,0:T(8,128)(2,1)} %blocks_ref.1) | copy-start | bytes 1572868
  51.4 28.5 %copy-start.7 = (bf16[16,256,128]{2,1,0:T(8,128)(2,1)S(1)}, bf16[16,256,128]{2,1,0:T(8,128)(2,1)}, u32[]{:S(2)}) copy-start(bf16[16,256,128]{2,1,0:T(8,128)(2,1)} %proj_ref.3) | copy-start | bytes 3145732
  66.2 13.6 %all-to-all-start.3 = ((bf16[16,8,512]{2,1,0:T(8,128)(2,1)}), bf16[16,8,512]{2,1,0:T(8,128)(2,1)S(1)}, u32[]{:S(2)}, u32[]{:S(2)}) async-start(bf16[16,8,512]{2,1,0:T(8,128)(2,1)} %bitcast.8), calls=%async_computation.3 | async-start | bytes 262144 | tf_op jit(solution)/shard_map/all_to_all | solution.py:294
where the time goes:
time: 83.2 us; the launch traced here: 82.5 us
  blocking collectives  36.9 us (44%)
  waiting for transfers between devices  17.2 us (21%)
  starting transfers between devices  13 us (16%)
  Pallas kernels  10.3 us (12%)
  local copies, waits for them, and re-layouts  4.8 us (6%)
    all_to_all x2, blocking collectives, swap(): lax.all_to_all(cells.reshape(parts, rows, -1), axis, 0, 0, tiled=True)  36.9 us
    all_to_all x2, waiting for transfers between devices, swap(): lax.all_to_all(cells.reshape(parts, rows, -1), axis, 0, 0, tiled=True)  17.2 us
    all_to_all x2, starting transfers between devices, swap(): lax.all_to_all(cells.reshape(parts, rows, -1), axis, 0, 0, tiled=True)  13 us
    unnamed x42, local copies, waits for them, and re-layouts  4.7 us
    pallas_call x1, Pallas kernels, body(): call(gather_kernel, [shape(2, SOURCES)], [VM, VM, SM, VM, VM, VM, VM], [p...  2.57 us
    pallas_call x1, Pallas kernels, body(): call(spread_kernel, [shape(128, CELLS, dtype=BF16), shape(128, SLOTS)], [...  2.05 us
    pallas_call x1, Pallas kernels, body(): call(x_kernel, [shape(512, 128, dtype=BF16)], [VM] * 6, [], 10 ** 9, 2 *...  1.99 us
  transfers between devices with their start and end apart: 2, of which 2 were waited for; matrix products, arithmetic and copies ran while one was open for 0% of the time, Pallas kernels for 1%

commit v1 on v0

v1 whole, which is shorter than its diff:
```python
import math

import jax
import jax.numpy as jnp
import ml_dtypes
import numpy as np
from jax import lax
from jax.experimental import pallas as pl
from jax.experimental.pallas import tpu as pltpu
from jax.sharding import PartitionSpec as P

TILES = 16
SLOTS = 128
PAIRS = 8
SOURCES = 1536
NU = 12
UPAD = 16
NV = 40
CELLS = 512
F32 = jnp.float32
BF16 = jnp.bfloat16
VMEM_LIMIT = 16 * 1024 * 1024
LIMIT_A = 65536 * 1024 - 960 * 1024


def split_table(table):
    high = table.astype(np.float32).astype(ml_dtypes.bfloat16)
    low = (table - high.astype(np.float64)).astype(np.float32).astype(ml_dtypes.bfloat16)
    return high, low


def as_real(theta, inverse):
    sign = -1.0 if inverse else 1.0
    cos, sin = np.cos(theta), sign * np.sin(theta)
    return np.stack([np.stack([cos, sin], -1), np.stack([-sin, cos], -1)], -2)


def z_tables():
    kz = np.arange(32)
    theta = 2.0 * np.pi * (np.outer(kz, kz) % 32) / 32
    forward = as_real(theta, False).reshape(16, 2, 32, 2, 2)
    table = np.einsum("jqzoc,hg->jhqogcz", forward, np.eye(2)).reshape(128, 128)
    backward = as_real(theta, True).reshape(16, 2, 32, 2, 2) / 32.0
    table_back = np.einsum("jqzoc,hg->jhqcgoz", backward, np.eye(2)).reshape(128, 128)
    first = np.zeros((4096, 256), ml_dtypes.bfloat16)
    p = np.arange(256)
    first[p, (p // 32 % 2) * 128 + (p // 64) * NV + p // 4 % 8] = 1.0
    first[256:384, 0:128], first[256:384, 128:256] = split_table(table)
    return jnp.asarray(first), in_rows(table_back)


def in_rows(*tables):
    padded = [np.pad(table, ((0, 0), (0, 128 - table.shape[1]))) for table in tables]
    return jnp.asarray(np.concatenate(padded, 0).astype(np.float32))


def y_tables():
    k = np.arange(16)
    theta = 2.0 * np.pi * (np.outer(k, k) % 16) / 16
    eyes = np.einsum("hg,qr->hgqr", np.eye(2), np.eye(2))
    table = np.einsum("kjoc,hgqr->jhqcgokr", as_real(theta, False), eyes).reshape(128, 128)
    table_back = np.einsum("kjoc,hgqr->jgrohckq", as_real(theta, True) / 512.0, eyes).reshape(128, 128)
    phi = 2.0 * np.pi * np.outer(np.arange(NV) - 4, k) / 512
    wide = np.broadcast_to(phi[:, None, None, :, None], (NV, 2, 2, 16, 2)).reshape(NV, 128)
    psi = 2.0 * np.pi * (np.outer(np.arange(32), np.arange(NV) - 4) % 32) / 32
    rows = np.concatenate([np.cos(psi), np.sin(psi)], 1)
    rows_back = np.concatenate([np.cos(psi.T), -np.sin(psi.T)], 1)
    turn = (np.cos(wide), np.sin(wide))
    return in_rows(*turn, table, rows), in_rows(*turn, table_back, rows_back)


def x_tables():
    k0 = np.arange(32)
    alpha = 2.0 * np.pi * (np.outer(k0, k0) % 32) / 32
    rows = np.concatenate([np.cos(alpha), np.sin(alpha)], 1)
    rows_back = np.concatenate([np.cos(alpha), -np.sin(alpha)], 1) / 512.0
    beta = 2.0 * np.pi * np.outer(k0, np.arange(NU) - 2) / 256
    phi = 2.0 * np.pi * (k0[:, None] + 32 * np.arange(8)[None, :]) / 512
    return in_rows(rows, rows_back, np.concatenate([np.cos(beta), np.sin(beta), np.cos(phi), np.sin(phi)], 1))


def mm(a, b):
    return lax.dot_general(a, b, (((1,), (0,)), ((), ())), preferred_element_type=F32)


def mm_nt(a, b):
    return lax.dot_general(a, b, (((1,), (1,)), ((), ())), preferred_element_type=F32)


def halves(value):
    high = value.astype(BF16)
    return high, (value - high.astype(F32)).astype(BF16)


def iota(shape, axis):
    return lax.broadcasted_iota(jnp.int32, shape, axis)


def turned(value):
    bit = (iota(value.shape, 1) // 32) % 2
    return jnp.where(bit == 0, pltpu.roll(value, 96, 1), -pltpu.roll(value, 32, 1))


def crossed(value):
    half = iota(value.shape, 1) // 64
    return pltpu.roll(value, 64, 1) + jnp.where(half == 0, value, -value)


def layer_picks(anchor):
    fan = jnp.where(iota((TILES, 256), 0) == (iota((TILES, 256), 1) // 8) % TILES, 1.0, 0.0).astype(BF16)
    low = mm(anchor[2:3, :].astype(F32).astype(BF16), fan)
    at = iota((1, 256), 1)
    want = low + ((at // 128) * 64 + ((at // 4) % 2) * 32 + at % 4).astype(F32)
    return jnp.where(iota((128, 256), 0) == want.astype(jnp.int32), 1.0, 0.0).astype(BF16)


def place(anchor_ref, t):
    x = (anchor_ref[0, t] & 15) + 1
    y = (anchor_ref[1, t] & 31) + 1
    starts = (((x + 1) >> 1) * NV + y, (x >> 1) * NV + y)
    return x & 1, starts


def as_row(slot):
    return jnp.concatenate([slot[r : r + 1, :] for r in range(SOURCES // 128)], axis=1)


def slot_picks(slot):
    return jnp.where(iota((SLOTS, SOURCES), 0) == (slot & 127), 1.0, 0.0).astype(BF16)


def spread_kernel(
    charges_hbm,
    slot_hbm,
    anchor_hbm,
    pairs_hbm,
    proj_hbm,
    tables_hbm,
    out_ref,
    slots_ref,
    ints_ref,
    charges_ref,
    slot_ref,
    anchor_ref,
    anchor_vec,
    pairs_vec,
    proj_ref,
    tables_ref,
    nodes,
    layers,
    patch,
    cells,
    sems,
):
    fetched = (
        (charges_hbm, charges_ref),
        (slot_hbm, slot_ref),
        (anchor_hbm, anchor_ref),
        (anchor_hbm, anchor_vec),
        (pairs_hbm, pairs_vec),
        (proj_hbm, proj_ref),
        (tables_hbm.at[0:384], tables_ref),
    )
    copies = [pltpu.make_async_copy(src, dst, sems.at[n]) for n, (src, dst) in enumerate(fetched)]
    for copy in copies:
        copy.start()
    cells[...] = jnp.zeros_like(cells)
    for copy in copies[:5]:
        copy.wait()
    ints_ref[...] = jnp.zeros_like(ints_ref)
    ints_ref[0 : SOURCES // 128, :] = slot_ref[...]
    ints_ref[16:19, 0:TILES] = anchor_vec[...]
    ints_ref[20:22, 0:PAIRS] = pairs_vec[...]
    slot = as_row(slot_ref[...])
    row = iota((32, SOURCES), 0)
    charge = jnp.where(row % 2 == 0, charges_ref[0:1, :], charges_ref[1:2, :])
    held = jnp.where(row // 2 == (slot >> 7), charge, 0.0).astype(BF16)
    slots_ref[...] = mm_nt(held, slot_picks(slot))
    picks = layer_picks(anchor_vec[...])
    copies[5].wait()
    for t in range(TILES):
        nodes[2 * t : 2 * t + 2, :] = mm_nt(slots_ref[2 * t : 2 * t + 2, :].astype(BF16), proj_ref[t])
    value = nodes[...]
    layer = iota((32, 128), 1) % 4
    for half in range(2):
        for b in range(4):
            part = value[:, 128 * half : 128 * half + 128]
            layers[pl.ds(128 * half + b, 32, stride=4), :] = jnp.where(layer == b, part, 0.0)
    high, low = halves(jnp.concatenate([layers[0:128, :], layers[128:256, :]], axis=1))
    copies[6].wait()
    spread = tables_ref[0:256, :]
    patch[...] = mm(high, spread) + mm(low, spread)
    empty = jnp.zeros((8, 128), F32)
    for t in range(TILES):
        odd, starts = place(anchor_ref, t)
        even_part = patch[8 * t : 8 * t + 8, 0:128]
        odd_part = patch[8 * t : 8 * t + 8, 128:256]
        parts = (jnp.where(odd == 1, odd_part, even_part), jnp.where(odd == 1, even_part, odd_part))
        for h in range(2):
            wide = jnp.concatenate([parts[h], empty], axis=1)
            wide = pltpu.roll(wide, starts[h] & 127, 1)
            lane = pl.multiple_of((starts[h] >> 7) * 128, 128)
            cells[128 * h + 8 * t : 128 * h + 8 * t + 8, pl.ds(lane, 256)] = wide
    phase_high = mm(tables_ref[256:384, 0:128], picks).astype(BF16)
    phase_low = mm(tables_ref[256:384, 128:256], picks).astype(BF16)
    high, low = halves(cells[...])
    out = mm(phase_high, high) + mm(phase_high, low) + mm(phase_low, high)
    out_ref[...] = out.astype(BF16)


def y_kernel(in_ref, table_ref, out_ref, hold):
    data = in_ref[...].astype(F32).T.astype(BF16)
    cos, sin = table_ref[0:NV, :], table_ref[NV : 2 * NV, :]
    table = table_ref[2 * NV : 2 * NV + 128, :]
    high, low = halves(jnp.concatenate([table, turned(table)], axis=1))
    both = mm(data, high) + mm(data, low)
    rows = halves(table_ref[2 * NV + 128 : 2 * NV + 160, 0 : 2 * NV])
    hold[...] = jnp.zeros_like(hold)
    for u in range(NU):
        plain = both[NV * u : NV * (u + 1), 0:128]
        turn = both[NV * u : NV * (u + 1), 128:256]
        lines = jnp.concatenate([plain * cos + turn * sin, turn * cos - plain * sin], axis=0)
        high, low = halves(lines)
        out = mm(rows[0], high) + mm(rows[0], low) + mm(rows[1], high)
        hold[pl.ds(u, 32, stride=UPAD), :] = out
    out_ref[...] = hold[...].astype(BF16)


def rotated(value, cos, sin):
    plain, turn = value
    return plain * cos + turn * sin, turn * cos - plain * sin


def eighths(value, count, sign):
    plain, turn = value
    if count == 0:
        return value
    if count == 2:
        return (turn, -plain) if sign > 0 else (-turn, plain)
    if count == 3:
        return eighths(eighths(value, 2, sign), 1, sign)
    root = math.sqrt(0.5)
    if sign > 0:
        return (plain + turn) * root, (turn - plain) * root
    return (plain - turn) * root, (turn + plain) * root


def short_dft(values, sign):
    count = len(values)
    if count == 1:
        return values
    even, odd = short_dft(values[0::2], sign), short_dft(values[1::2], sign)
    odd = [eighths(value, 8 // count * n, sign) for n, value in enumerate(odd)]
    sums = [(a[0] + b[0], a[1] + b[1]) for a, b in zip(even, odd)]
    return sums + [(a[0] - b[0], a[1] - b[1]) for a, b in zip(even, odd)]


def line_pair(rows, plain, turn):
    four = jnp.concatenate(
        [jnp.concatenate([plain, turn], axis=1), jnp.concatenate([turn, -plain], axis=1)], axis=0
    ).astype(BF16)
    return mm(rows[0], four) + mm(rows[1], four)


def x_kernel(in_ref, real_ref, imag_ref, table_ref, out_ref, hold, hold_turned):
    into = halves(table_ref[0:32, 0:64])
    back = halves(table_ref[32:64, 0:64])
    angles = table_ref[64:96, :]
    second = iota((32, 128), 1) >= 64

    def step(u):
        shape = (32, 128)
        cos, sin = angles[:, u : u + 1], angles[:, NU + u : NU + u + 1]
        return jnp.broadcast_to(cos, shape), jnp.broadcast_to(sin, shape)

    def fold(n):
        n = n + 2 * NU
        return jnp.where(second, angles[:, n : n + 1], 1.0), jnp.where(second, angles[:, n + 8 : n + 9], 0.0)

    data = in_ref[...].astype(F32)
    hold[...] = data
    hold_turned[...] = turned(data)
    classes = [None] * 8
    for u in range(NU):
        plain = hold[pl.ds(u, 32, stride=UPAD), :]
        both = line_pair(into, plain, hold_turned[pl.ds(u, 32, stride=UPAD), :])
        value = rotated((both[:, 0:128], both[:, 128:256]), *step(u))
        at = (u - 2) % 8
        classes[at] = value if classes[at] is None else tuple(a + b for a, b in zip(classes[at], value))
    lines = short_dft(classes, 1)

    def wide(green):
        green = green.reshape(32, 512)
        first, second = green[:, 0:256], green[:, 256:512]
        return jnp.concatenate([first, first, second, second], axis=0).T

    real, imag = wide(real_ref[...]), wide(imag_ref[...])
    for n in range(8):
        rows = slice(32 * n, 32 * n + 32)
        cos, sin = fold(n)
        plain, turn = rotated(lines[n], cos, sin)
        plain, turn = crossed(plain), crossed(turn)
        plain, turn = plain * real[rows] - turn * imag[rows], turn * real[rows] + plain * imag[rows]
        lines[n] = rotated((crossed(plain), crossed(turn)), cos, -sin)
    classes = short_dft(lines, -1)
    for u in range(NU):
        cos, sin = step(u)
        value = rotated(classes[(u - 2) % 8], cos, -sin)
        high, low = halves(jnp.concatenate(value, axis=0))
        out = mm(back[0], high) + mm(back[0], low) + mm(back[1], high)
        hold[pl.ds(u, 32, stride=UPAD), :] = out
    out_ref[...] = hold[...].astype(BF16)


def y_back_kernel(in_ref, table_ref, out_ref, hold, hold_turned):
    data = in_ref[...].astype(F32)
    hold[...] = data
    hold_turned[...] = turned(data)
    cos, sin = table_ref[0:NV, :], table_ref[NV : 2 * NV, :]
    tab = halves(table_ref[2 * NV : 2 * NV + 128, :])
    rows = halves(table_ref[2 * NV + 128 : 3 * NV + 128, 0:64])
    lines = []
    for u in range(NU):
        plain = hold[pl.ds(u, 32, stride=UPAD), :]
        turn = hold_turned[pl.ds(u, 32, stride=UPAD), :]
        both = line_pair(rows, plain, turn)
        lines.append(both[:, 0:128] * cos - both[:, 128:256] * sin)
    lines.append(jnp.zeros((CELLS - NU * NV, 128), F32))
    high, low = halves(jnp.concatenate(lines, axis=0))
    out = mm_nt(tab[0], high) + mm_nt(tab[0], low) + mm_nt(tab[1], high)
    out_ref[...] = out.astype(BF16)


def node_lanes():
    node = iota((256, 256), 0)
    lane = ((node >> 5) & 1) * 128 + (node >> 6) * NV + ((node >> 2) & 7)
    return jnp.where(iota((256, 256), 1) == lane, 1.0, 0.0).astype(BF16)


def gather_kernel(
    in_ref,
    ints_ref,
    proj_ref,
    slots_ref,
    blocks_ref,
    table_ref,
    out_ref,
    anchor_ref,
    cells,
    patch,
    layers,
    nodes,
    near,
    total,
    sem,
):
    copy = pltpu.make_async_copy(ints_ref.at[16:24], anchor_ref, sem)
    copy.start()
    near[...] = jnp.zeros_like(near)
    picks = layer_picks(ints_ref[16:19, 0:TILES])
    tab = halves(table_ref[...])
    phase_high = mm(tab[0], picks).T.astype(BF16)
    phase_low = mm(tab[1], picks).T.astype(BF16)
    data = in_ref[...]
    field = mm(phase_high, data) + mm(phase_low, data)
    cells[...] = field.astype(BF16).astype(F32)
    copy.wait()
    sign = jnp.where(iota((2, 128), 0) == 0, -1.0, 1.0)
    for q in range(8):
        source = slots_ref[pl.ds(anchor_ref[5, q] * 2, 2), :]
        turn = jnp.concatenate([source[1:2], source[0:1]], axis=0) * sign
        value = mm_nt(source.astype(BF16), blocks_ref[q, 0]) + mm_nt(turn.astype(BF16), blocks_ref[q, 1])
        target = pl.ds(anchor_ref[4, q] * 2, 2)
        near[target, :] = near[target, :] + value
    for t in range(TILES):
        odd, starts = place(anchor_ref, t)
        parts = []
        for h in range(2):
            lane = pl.multiple_of((starts[h] >> 7) * 128, 128)
            wide = cells[128 * h + 8 * t : 128 * h + 8 * t + 8, pl.ds(lane, 256)]
            parts.append(pltpu.roll(wide, (256 - (starts[h] & 127)) & 255, 1)[:, 0:128])
        patch[8 * t : 8 * t + 8, 0:128] = jnp.where(odd == 1, parts[1], parts[0])
        patch[8 * t : 8 * t + 8, 128:256] = jnp.where(odd == 1, parts[0], parts[1])
    value = mm_nt(patch[...].astype(BF16), node_lanes())
    layers[0:128, :] = value[:, 0:128]
    layers[128:256, :] = value[:, 128:256]
    layer = iota((32, 128), 1) % 4
    for half in range(2):
        value = layers[pl.ds(128 * half, 32, stride=4), :]
        for b in range(1, 4):
            value = jnp.where(layer == b, layers[pl.ds(128 * half + b, 32, stride=4), :], value)
        nodes[:, 128 * half : 128 * half + 128] = value
    for t in range(TILES):
        total[2 * t : 2 * t + 2, :] = mm(nodes[2 * t : 2 * t + 2, :].astype(BF16), proj_ref[t])
    high, low = halves(total[...] + near[...])
    slot = as_row(ints_ref[0 : SOURCES // 128, :])
    pick = slot_picks(slot)
    value = mm(high, pick) + mm(low, pick)
    value = jnp.where(iota((32, SOURCES), 0) // 2 == (slot >> 7), value, 0.0)
    value = value[0:8] + value[8:16] + value[16:24] + value[24:32]
    value = value + pltpu.roll(value, 4, 0)
    value = value + pltpu.roll(value, 2, 0)
    out_ref[...] = value[0:2]


VM = pl.BlockSpec(memory_space=pltpu.VMEM)
HB = pl.BlockSpec(memory_space=pltpu.HBM)


def call(kernel, outs, in_specs, scratch, flops, moved, limit=VMEM_LIMIT):
    return pl.pallas_call(
        kernel,
        out_shape=[shape(*out.shape, dtype=out.dtype) for out in outs],
        in_specs=in_specs,
        out_specs=[VM] * len(outs),
        scratch_shapes=scratch,
        compiler_params=pltpu.CompilerParams(vmem_limit_bytes=limit),
        cost_estimate=pl.CostEstimate(flops=flops, bytes_accessed=moved, transcendentals=0),
    )


def shape(*dims, dtype=F32):
    return jax.ShapeDtypeStruct(dims, dtype)


def swap(cells, axis, rows):
    parts = lax.axis_size(axis)
    moved = lax.all_to_all(cells.reshape(parts, rows, -1), axis, 0, 0, tiled=True)
    return moved.reshape(parts * rows, -1)


def body(charges, source_slot, tile_anchor, projection, near_pairs, near_blocks, green_real, green_imag):
    first, z_back = z_tables()
    y_table, y_back = y_tables()
    block = pltpu.VMEM((512, 128), F32)
    cells, slots, ints = call(
        spread_kernel,
        [shape(128, CELLS, dtype=BF16), shape(32, SLOTS), shape(24, 128, dtype=jnp.int32)],
        [HB] * 6,
        [
            pltpu.VMEM((2, SOURCES), F32),
            pltpu.VMEM((SOURCES // 128, 128), jnp.int32),
            pltpu.SMEM((3, TILES), jnp.int32),
            pltpu.VMEM((3, TILES), jnp.int32),
            pltpu.VMEM((2, PAIRS), jnp.int32),
            pltpu.VMEM((TILES, 256, SLOTS), BF16),
            pltpu.VMEM((384, 256), BF16),
            pltpu.VMEM((32, 256), F32),
            pltpu.VMEM((256, 128), F32),
            pltpu.VMEM((128, 256), F32),
            pltpu.VMEM((256, CELLS), F32),
            pltpu.SemaphoreType.DMA((7,)),
        ],
        10**9,
        2 * 10**6,
        LIMIT_A,
    )(charges, source_slot.reshape(SOURCES // 128, 128), tile_anchor.T, near_pairs.T, projection, first)
    cells = swap(cells, "gy", 8)
    lines = shape(512, 128, dtype=BF16)
    lines = call(y_kernel, [lines], [VM] * 2, [block], 10**8, 10**6)(cells, y_table)[0]
    lines = swap(lines, "gx", UPAD)
    lines = call(x_kernel, [lines], [VM] * 4, [block] * 2, 10**8, 10**6)(
        lines, green_real.transpose(1, 2, 0), green_imag.transpose(1, 2, 0), x_tables()
    )[0]
    lines = swap(lines, "gx", UPAD)
    cells = call(y_back_kernel, [cells], [VM] * 2, [block] * 2, 10**8, 10**6)(lines, y_back)[0]
    cells = swap(cells, "gy", 8)
    return call(
        gather_kernel,
        [shape(2, SOURCES)],
        [VM] * 6,
        [
            pltpu.SMEM((8, 128), jnp.int32),
            pltpu.VMEM((256, CELLS), F32),
            pltpu.VMEM((128, 256), F32),
            pltpu.VMEM((256, 128), F32),
            pltpu.VMEM((32, 256), F32),
            pltpu.VMEM((32, SLOTS), F32),
            pltpu.VMEM((32, SLOTS), F32),
            pltpu.SemaphoreType.DMA,
        ],
        10**9,
        2 * 10**6,
    )(cells, ints, projection, slots, near_blocks, z_back)[0]


def solution(mesh):
    return jax.shard_map(
        body,
        mesh=mesh,
        in_specs=(
            P(None, ("gx", "gy")),
            P(("gx", "gy")),
            P(("gx", "gy"), None),
            P(("gx", "gy"), None, None),
            P(("gx", "gy"), None),
            P(("gx", "gy"), None, None, None),
            P(None, "gx", "gy"),
            P(None, "gx", "gy"),
        ),
        out_specs=P(None, ("gx", "gy")),
        check_vma=False,
    )
```

time: 83.2 us -> 76.7 us (0.922)
  blocking collectives: 36.9 us -> 67.9 us
  waiting for transfers between devices: 17.2 us -> 0 us
  starting transfers between devices: 13 us -> 0 us
  local copies, waits for them, and re-layouts: 4.8 us -> 0.05 us
  Pallas kernels: 10.3 us -> 8.08 us
    all_to_all x2 -> x4, blocking collectives: 36.9 us -> 67.9 us  [swap(): lax.all_to_all(cells.reshape(parts, rows, -1), axis, 0, 0, tiled=True)]
    all_to_all x2 -> x0, waiting for transfers between devices: 17.2 us -> none  [swap(): lax.all_to_all(cells.reshape(parts, rows, -1), axis, 0, 0, tiled=True)]
    all_to_all x2 -> x0, starting transfers between devices: 13 us -> none  [swap(): lax.all_to_all(cells.reshape(parts, rows, -1), axis, 0, 0, tiled=True)]
    unnamed x42 -> x20, local copies, waits for them, and re-layouts: 4.7 us -> 0.05 us
    pallas_call x6 -> x5, Pallas kernels: 10.3 us -> 8.08 us  [the longest x1 3.23 us: body(): call(spread_kernel, [shape(128, CELLS, dtype=BF16), shape(32, SLOTS), sha...]
  transfers between devices with their start and end apart: 2 -> 0, of which waited for: 2 -> 0; matrix products, arithmetic and copies ran while one was open for 0% -> 0% of each run, Pallas kernels for 1% -> 0%
where the time goes in v1:
time: 76.7 us; the launch traced here: 76.1 us
  blocking collectives  67.9 us (89%)
  Pallas kernels  8.08 us (11%)
    all_to_all x4, blocking collectives, swap(): lax.all_to_all(cells.reshape(parts, rows, -1), axis, 0, 0, tiled=True)  67.9 us
    pallas_call x1, Pallas kernels, body(): call(spread_kernel, [shape(128, CELLS, dtype=BF16), shape(32, SLOTS), sha...  3.23 us
    pallas_call x1, Pallas kernels, body(): call(gather_kernel, [shape(2, SOURCES)], [VM] * 6, [pltpu.SMEM((8, 128),...  2.26 us

profile of v1, /device:TPU:1, one launch (start us, length us, event | category | flops | bytes accessed | tf_op | source)
XLA Modules:
  0.0 76.1 jit_solution(4779299083894070191)
XLA Ops:
  0.0 0.0 copy-start.1
  0.0 0.0 copy-start.2
  0.0 0.0 copy-start.3
  0.0 0.0 copy-start.4
  0.0 0.0 copy-start
  0.0 0.0 copy-start.7
  0.0 3.2 %shard_map.127 = (bf16[128,512]{1,0:T(8,128)(2,1)}, f32[32,128]{1,0:T(8,128)}, s32[24,128]{1,0:T(8,128)}) custom-call(f32[2,1536]{1,0:T(2,128)} %charges_hbm.1, s32[12,128]{1,0:T(8,128)} %bitcast.23, s32[3,16]{1,0:T(4,128)} %bitcast.24, s32[2,8]{1,0:T(2,128)} %bitcast.25, bf16[16,256,128]{2,1,0:T(8,128)(2,1)} %proj_ref.1, ...), custom_call_target="tpu_custom_call" | custom-call | flops 1000000000 | bytes 2000000 | tf_op jit(solution)/shard_map/pallas_call | solution.py:436
  3.3 0.0 copy-start.5
  3.3 0.0 copy-start.6
  3.3 0.0 copy-start.8
  3.3 0.0 copy-start.9
  3.3 23.5 %all_to_all.20 = bf16[16,8,512]{2,1,0:T(8,128)(2,1)S(1)} all-to-all(bf16[16,8,512]{2,1,0:T(8,128)(2,1)} %bitcast.22), channel_id=1, replica_groups=mesh['gx'=32,'gy'=16] {'gy'}, dimensions={0} | all-to-all | bytes 262144 | tf_op jit(solution)/shard_map/all_to_all | solution.py:428
  26.9 0.0 copy-done.1
  26.9 0.8 %shard_map.128 = bf16[512,128]{1,0:T(8,128)(2,1)S(1)} custom-call(bf16[128,512]{1,0:T(8,128)(2,1)S(1)} %bitcast.13, f32[240,128]{1,0:T(8,128)S(1)} %copy-done.1), custom_call_target="tpu_custom_call" | custom-call | flops 100000000 | bytes 1000000 | tf_op jit(solution)/shard_map/pallas_call | solution.py:460
  27.7 18.3 %all_to_all.21 = bf16[32,16,128]{2,1,0:T(8,128)(2,1)S(1)} all-to-all(bf16[32,16,128]{2,1,0:T(8,128)(2,1)S(1)} %bitcast.14), channel_id=1, replica_groups=mesh['gx'=32,'gy'=16] {'gx'}, dimensions={0} | all-to-all | bytes 262144 | tf_op jit(solution)/shard_map/all_to_all | solution.py:428
  46.0 0.0 copy-done.2
  46.0 0.0 copy-done.3
  46.0 0.0 copy-done.4
  46.0 1.1 %shard_map.129 = bf16[512,128]{1,0:T(8,128)(2,1)S(1)} custom-call(bf16[512,128]{1,0:T(8,128)(2,1)S(1)} %bitcast.15, f32[16,2,512]{2,1,0:T(2,128)S(1)} %bitcast.20, f32[16,2,512]{2,1,0:T(2,128)S(1)} %bitcast.21, f32[96,128]{1,0:T(8,128)S(1)} %copy-done.4), custom_call_target="tpu_custom_call" | custom-call | flops 100000000 | bytes 1000000 | tf_op jit(solution)/shard_map/pallas_call | solution.py:462
  47.1 13.4 %all_to_all.22 = bf16[32,16,128]{2,1,0:T(8,128)(2,1)S(1)} all-to-all(bf16[32,16,128]{2,1,0:T(8,128)(2,1)S(1)} %bitcast.16), channel_id=1, replica_groups=mesh['gx'=32,'gy'=16] {'gx'}, dimensions={0} | all-to-all | bytes 262144 | tf_op jit(solution)/shard_map/all_to_all | solution.py:428
  60.5 0.0 copy-done
  60.5 0.7 shard_map.130
  61.2 12.6 %all_to_all.23 = bf16[16,8,512]{2,1,0:T(8,128)(2,1)S(1)} all-to-all(bf16[16,8,512]{2,1,0:T(8,128)(2,1)S(1)} %bitcast.18), channel_id=1, replica_groups=mesh['gx'=32,'gy'=16] {'gy'}, dimensions={0} | all-to-all | bytes 262144 | tf_op jit(solution)/shard_map/all_to_all | solution.py:428
  73.8 0.0 copy-done.7
  73.8 0.0 copy-done.5
  73.8 0.0 copy-done.6
  73.8 0.0 copy-done.8
  73.8 0.0 copy-done.9
  73.8 2.3 %shard_map.131 = f32[2,1536]{1,0:T(2,128)} custom-call(bf16[128,512]{1,0:T(8,128)(2,1)S(1)} %bitcast.19, s32[24,128]{1,0:T(8,128)S(1)} %copy-done.9, bf16[16,256,128]{2,1,0:T(8,128)(2,1)S(1)} %copy-done.5, f32[32,128]{1,0:T(8,128)S(1)} %copy-done.8, bf16[8,2,128,128]{3,2,1,0:T(8,128)(2,1)S(1)} %copy-done.6, f32[128,128]{1,0:T(8,128)S(1)} %copy-done.7), custom_call_target="tpu_custom_call" | custom-call | flops 1000000000 | bytes 2000000 | tf_op jit(solution)/shard_map/pallas_call | solution.py:468
Async XLA Ops:
  0.0 26.9 %copy-start.1 = (f32[240,128]{1,0:T(8,128)S(1)}, f32[240,128]{1,0:T(8,128)}, u32[]{:S(2)}) copy-start(f32[240,128]{1,0:T(8,128)} %constant.12.clone.table_ref) | copy-start | bytes 368644
  0.0 46.0 %copy-start.2 = (f32[512,16,2]{0,2,1:T(2,128)S(1)}, f32[512,16,2]{0,2,1:T(2,128)}, u32[]{:S(2)}) copy-start(f32[512,16,2]{0,2,1:T(2,128)} %param.19) | copy-start | bytes 196612
  0.0 46.0 %copy-start.3 = (f32[512,16,2]{0,2,1:T(2,128)S(1)}, f32[512,16,2]{0,2,1:T(2,128)}, u32[]{:S(2)}) copy-start(f32[512,16,2]{0,2,1:T(2,128)} %param.20) | copy-start | bytes 196612
  0.0 46.0 %copy-start.4 = (f32[96,128]{1,0:T(8,128)S(1)}, f32[96,128]{1,0:T(8,128)}, u32[]{:S(2)}) copy-start(f32[96,128]{1,0:T(8,128)} %constant.14.clone.table_ref) | copy-start | bytes 147460
  0.0 60.5 %copy-start = (f32[248,128]{1,0:T(8,128)S(1)}, f32[248,128]{1,0:T(8,128)}, u32[]{:S(2)}) copy-start(f32[248,128]{1,0:T(8,128)} %constant.13.clone.table_ref) | copy-start | bytes 380932
  0.0 73.8 %copy-start.7 = (f32[128,128]{1,0:T(8,128)S(1)}, f32[128,128]{1,0:T(8,128)}, u32[]{:S(2)}) copy-start(f32[128,128]{1,0:T(8,128)} %constant.11.clone.table_ref) | copy-start | bytes 196612
  3.3 70.5 %copy-start.5 = (bf16[16,256,128]{2,1,0:T(8,128)(2,1)S(1)}, bf16[16,256,128]{2,1,0:T(8,128)(2,1)}, u32[]{:S(2)}) copy-start(bf16[16,256,128]{2,1,0:T(8,128)(2,1)} %proj_ref.1) | copy-start | bytes 3145732
  3.3 70.5 %copy-start.6 = (bf16[8,2,128,128]{3,2,1,0:T(8,128)(2,1)S(1)}, bf16[8,2,128,128]{3,2,1,0:T(8,128)(2,1)}, u32[]{:S(2)}) copy-start(bf16[8,2,128,128]{3,2,1,0:T(8,128)(2,1)} %blocks_ref.1) | copy-start | bytes 1572868
  3.3 70.5 %copy-start.8 = (f32[32,128]{1,0:T(8,128)S(1)}, f32[32,128]{1,0:T(8,128)}, u32[]{:S(2)}) copy-start(f32[32,128]{1,0:T(8,128)} %get-tuple-element.10.slots_ref) | copy-start | bytes 49156
  3.3 70.5 %copy-start.9 = (s32[24,128]{1,0:T(8,128)S(1)}, s32[24,128]{1,0:T(8,128)}, u32[]{:S(2)}) copy-start(s32[24,128]{1,0:T(8,128)} %get-tuple-element.9.ints_ref) | copy-start | bytes 36868

commit v2 on v1

--- a/solution.py
+++ b/solution.py
@@ -14,7 +14,9 @@
 PAIRS = 8
 SOURCES = 1536
 NU = 12
-UPAD = 16
+LINES = (96, 4, 128)
+ORDER_X = (1, 10, 13, 25, 21, 8, 15, 26, 7, 0, 28, 18, 6, 4, 20, 24, 12, 16, 3, 2, 31, 14, 23, 29, 5, 11, 17, 27, 30, 22, 9, 19)
+ORDER_Y = tuple(2 * z + x for x in range(2) for z in range(8))
 NV = 40
 CELLS = 512
 F32 = jnp.float32
@@ -38,9 +40,9 @@
 def z_tables():
     kz = np.arange(32)
     theta = 2.0 * np.pi * (np.outer(kz, kz) % 32) / 32
-    forward = as_real(theta, False).reshape(16, 2, 32, 2, 2)
+    forward = as_real(theta, False).reshape(16, 2, 32, 2, 2)[list(ORDER_Y)]
     table = np.einsum("jqzoc,hg->jhqogcz", forward, np.eye(2)).reshape(128, 128)
-    backward = as_real(theta, True).reshape(16, 2, 32, 2, 2) / 32.0
+    backward = as_real(theta, True).reshape(16, 2, 32, 2, 2)[list(ORDER_Y)] / 32.0
     table_back = np.einsum("jqzoc,hg->jhqcgoz", backward, np.eye(2)).reshape(128, 128)
     first = np.zeros((4096, 256), ml_dtypes.bfloat16)
     p = np.arange(256)
@@ -56,13 +58,13 @@
 
 def y_tables():
     k = np.arange(16)
-    theta = 2.0 * np.pi * (np.outer(k, k) % 16) / 16
+    theta = 2.0 * np.pi * (np.outer(k, np.array(ORDER_Y)) % 16) / 16
     eyes = np.einsum("hg,qr->hgqr", np.eye(2), np.eye(2))
     table = np.einsum("kjoc,hgqr->jhqcgokr", as_real(theta, False), eyes).reshape(128, 128)
     table_back = np.einsum("kjoc,hgqr->jgrohckq", as_real(theta, True) / 512.0, eyes).reshape(128, 128)
     phi = 2.0 * np.pi * np.outer(np.arange(NV) - 4, k) / 512
     wide = np.broadcast_to(phi[:, None, None, :, None], (NV, 2, 2, 16, 2)).reshape(NV, 128)
-    psi = 2.0 * np.pi * (np.outer(np.arange(32), np.arange(NV) - 4) % 32) / 32
+    psi = 2.0 * np.pi * (np.outer(np.array(ORDER_X), np.arange(NV) - 4) % 32) / 32
     rows = np.concatenate([np.cos(psi), np.sin(psi)], 1)
     rows_back = np.concatenate([np.cos(psi.T), -np.sin(psi.T)], 1)
     turn = (np.cos(wide), np.sin(wide))
@@ -71,9 +73,9 @@
 
 def x_tables():
     k0 = np.arange(32)
-    alpha = 2.0 * np.pi * (np.outer(k0, k0) % 32) / 32
+    alpha = 2.0 * np.pi * (np.outer(k0, np.array(ORDER_X)) % 32) / 32
     rows = np.concatenate([np.cos(alpha), np.sin(alpha)], 1)
-    rows_back = np.concatenate([np.cos(alpha), -np.sin(alpha)], 1) / 512.0
+    rows_back = np.concatenate([np.cos(alpha.T), -np.sin(alpha.T)], 1) / 512.0
     beta = 2.0 * np.pi * np.outer(k0, np.arange(NU) - 2) / 256
     phi = 2.0 * np.pi * (k0[:, None] + 32 * np.arange(8)[None, :]) / 512
     return in_rows(rows, rows_back, np.concatenate([np.cos(beta), np.sin(beta), np.cos(phi), np.sin(phi)], 1))
@@ -215,15 +217,14 @@
     high, low = halves(jnp.concatenate([table, turned(table)], axis=1))
     both = mm(data, high) + mm(data, low)
     rows = halves(table_ref[2 * NV + 128 : 2 * NV + 160, 0 : 2 * NV])
-    hold[...] = jnp.zeros_like(hold)
     for u in range(NU):
         plain = both[NV * u : NV * (u + 1), 0:128]
         turn = both[NV * u : NV * (u + 1), 128:256]
         lines = jnp.concatenate([plain * cos + turn * sin, turn * cos - plain * sin], axis=0)
         high, low = halves(lines)
         out = mm(rows[0], high) + mm(rows[0], low) + mm(rows[1], high)
-        hold[pl.ds(u, 32, stride=UPAD), :] = out
-    out_ref[...] = hold[...].astype(BF16)
+        hold[pl.ds(u, 32, stride=NU), :] = out
+    out_ref[...] = hold[...].reshape(LINES).astype(BF16)
 
 
 def rotated(value, cos, sin):
@@ -277,13 +278,13 @@
         n = n + 2 * NU
         return jnp.where(second, angles[:, n : n + 1], 1.0), jnp.where(second, angles[:, n + 8 : n + 9], 0.0)
 
-    data = in_ref[...].astype(F32)
+    data = in_ref[...].astype(F32).reshape(384, 128)
     hold[...] = data
     hold_turned[...] = turned(data)
     classes = [None] * 8
     for u in range(NU):
-        plain = hold[pl.ds(u, 32, stride=UPAD), :]
-        both = line_pair(into, plain, hold_turned[pl.ds(u, 32, stride=UPAD), :])
+        plain = hold[pl.ds(u, 32, stride=NU), :]
+        both = line_pair(into, plain, hold_turned[pl.ds(u, 32, stride=NU), :])
         value = rotated((both[:, 0:128], both[:, 128:256]), *step(u))
         at = (u - 2) % 8
         classes[at] = value if classes[at] is None else tuple(a + b for a, b in zip(classes[at], value))
@@ -308,12 +309,12 @@
         value = rotated(classes[(u - 2) % 8], cos, -sin)
         high, low = halves(jnp.concatenate(value, axis=0))
         out = mm(back[0], high) + mm(back[0], low) + mm(back[1], high)
-        hold[pl.ds(u, 32, stride=UPAD), :] = out
-    out_ref[...] = hold[...].astype(BF16)
+        hold[pl.ds(u, 32, stride=NU), :] = out
+    out_ref[...] = hold[...].reshape(LINES).astype(BF16)
 
 
 def y_back_kernel(in_ref, table_ref, out_ref, hold, hold_turned):
-    data = in_ref[...].astype(F32)
+    data = in_ref[...].astype(F32).reshape(384, 128)
     hold[...] = data
     hold_turned[...] = turned(data)
     cos, sin = table_ref[0:NV, :], table_ref[NV : 2 * NV, :]
@@ -321,8 +322,8 @@
     rows = halves(table_ref[2 * NV + 128 : 3 * NV + 128, 0:64])
     lines = []
     for u in range(NU):
-        plain = hold[pl.ds(u, 32, stride=UPAD), :]
-        turn = hold_turned[pl.ds(u, 32, stride=UPAD), :]
+        plain = hold[pl.ds(u, 32, stride=NU), :]
+        turn = hold_turned[pl.ds(u, 32, stride=NU), :]
         both = line_pair(rows, plain, turn)
         lines.append(both[:, 0:128] * cos - both[:, 128:256] * sin)
     lines.append(jnp.zeros((CELLS - NU * NV, 128), F32))
@@ -423,16 +424,18 @@
     return jax.ShapeDtypeStruct(dims, dtype)
 
 
-def swap(cells, axis, rows):
+def swap(cells, axis):
     parts = lax.axis_size(axis)
-    moved = lax.all_to_all(cells.reshape(parts, rows, -1), axis, 0, 0, tiled=True)
-    return moved.reshape(parts * rows, -1)
+    blocks = cells.reshape((parts, -1) + cells.shape[1:] if cells.ndim == 3 else (parts, 8, -1))
+    order = ORDER_X if axis == "gx" else ORDER_Y
+    moved = lax.all_to_all(blocks, axis, 0, 0, axis_index_groups=[list(order)], tiled=True)
+    return moved.reshape(cells.shape)
 
 
 def body(charges, source_slot, tile_anchor, projection, near_pairs, near_blocks, green_real, green_imag):
     first, z_back = z_tables()
     y_table, y_back = y_tables()
-    block = pltpu.VMEM((512, 128), F32)
+    block = pltpu.VMEM((384, 128), F32)
     cells, slots, ints = call(
         spread_kernel,
         [shape(128, CELLS, dtype=BF16), shape(32, SLOTS), shape(24, 128, dtype=jnp.int32)],
@@ -455,16 +458,16 @@
         2 * 10**6,
         LIMIT_A,
     )(charges, source_slot.reshape(SOURCES // 128, 128), tile_anchor.T, near_pairs.T, projection, first)
-    cells = swap(cells, "gy", 8)
-    lines = shape(512, 128, dtype=BF16)
-    lines = call(y_kernel, [lines], [VM] * 2, [block], 10**8, 10**6)(cells, y_table)[0]
-    lines = swap(lines, "gx", UPAD)
-    lines = call(x_kernel, [lines], [VM] * 4, [block] * 2, 10**8, 10**6)(
+    cells = swap(cells, "gy")
+    lines = shape(*LINES, dtype=BF16)
+    lines = call(y_kernel, [lines], [VM] * 2, [block], 10**9, 10**6)(cells, y_table)[0]
+    lines = swap(lines, "gx")
+    lines = call(x_kernel, [lines], [VM] * 4, [block] * 2, 10**9, 10**6)(
         lines, green_real.transpose(1, 2, 0), green_imag.transpose(1, 2, 0), x_tables()
     )[0]
-    lines = swap(lines, "gx", UPAD)
-    cells = call(y_back_kernel, [cells], [VM] * 2, [block] * 2, 10**8, 10**6)(lines, y_back)[0]
-    cells = swap(cells, "gy", 8)
+    lines = swap(lines, "gx")
+    cells = call(y_back_kernel, [cells], [VM] * 2, [block] * 2, 10**9, 10**6)(lines, y_back)[0]
+    cells = swap(cells, "gy")
     return call(
         gather_kernel,
         [shape(2, SOURCES)],

time: 76.7 us -> 72.9 us (0.950)
  blocking collectives: 67.9 us -> 64.1 us
    all_to_all x4, blocking collectives: 67.9 us -> 64.1 us  [swap(): lax.all_to_all(blocks, axis, 0, 0, axis_index_groups=[list(order)], tiled...]
where the time goes in v2:
time: 72.9 us; the launch traced here: 72.3 us
  blocking collectives  64.1 us (88%)
  Pallas kernels  8.01 us (11%)
    all_to_all x4, blocking collectives, swap(): lax.all_to_all(blocks, axis, 0, 0, axis_index_groups=[list(order)], tiled...  64.1 us
    pallas_call x1, Pallas kernels, body(): call(spread_kernel, [shape(128, CELLS, dtype=BF16), shape(32, SLOTS), sha...  3.21 us
    pallas_call x1, Pallas kernels, body(): call(gather_kernel, [shape(2, SOURCES)], [VM] * 6, [pltpu.SMEM((8, 128),...  2.26 us

profile of v2, /device:TPU:1, one launch (start us, length us, event | category | flops | bytes accessed | tf_op | source)
XLA Modules:
  0.0 72.3 jit_solution(17617831078011009613)
XLA Ops:
  0.0 0.0 copy-start.5
  0.0 3.2 %shard_map.127 = (bf16[128,512]{1,0:T(8,128)(2,1)}, f32[32,128]{1,0:T(8,128)}, s32[24,128]{1,0:T(8,128)}) custom-call(f32[2,1536]{1,0:T(2,128)} %charges_hbm.1, s32[12,128]{1,0:T(8,128)} %bitcast.23, s32[3,16]{1,0:T(4,128)} %bitcast.24, s32[2,8]{1,0:T(2,128)} %bitcast.25, bf16[16,256,128]{2,1,0:T(8,128)(2,1)} %proj_ref.1, ...), custom_call_target="tpu_custom_call" | custom-call | flops 1000000000 | bytes 2000000 | tf_op jit(solution)/shard_map/pallas_call | solution.py:439
  3.2 0.0 copy-start.2
  3.2 0.0 copy-start.3
  3.2 0.0 copy-start.7
  3.3 22.6 %all_to_all.20 = bf16[16,8,512]{2,1,0:T(8,128)(2,1)S(1)} all-to-all(bf16[16,8,512]{2,1,0:T(8,128)(2,1)} %bitcast.22), channel_id=1, replica_groups={{0,2,4,6,8,10,12,14,1,3,5,7,9,11,13,15},{16,18,20,22,24,26,28,30,17,19,..., dimensions={0} | all-to-all | bytes 262144 | tf_op jit(solution)/shard_map/all_to_all | solution.py:431
  25.9 0.0 copy-done.5
  25.9 0.8 %shard_map.128 = bf16[96,4,128]{2,1,0:T(4,128)(2,1)S(1)} custom-call(bf16[128,512]{1,0:T(8,128)(2,1)S(1)} %bitcast.14, f32[240,128]{1,0:T(8,128)S(1)} %copy-done.5), custom_call_target="tpu_custom_call" | custom-call | flops 1000000000 | bytes 1000000 | tf_op jit(solution)/shard_map/pallas_call | solution.py:463
  26.7 0.0 copy-start.4
  26.7 17.5 %all_to_all.21 = bf16[32,3,4,128]{3,2,1,0:T(4,128)(2,1)S(1)} all-to-all(bf16[32,3,4,128]{3,2,1,0:T(4,128)(2,1)S(1)} %bitcast.16), channel_id=1, replica_groups={{16,160,208,400,336,128,240,416,112,0,448,288,96,64,320,384,192,256,48,..., dimensions={0} | all-to-all | bytes 196608 | tf_op jit(solution)/shard_map/all_to_all | solution.py:431
  44.2 0.0 copy-done.2
  44.2 0.0 copy-done.3
  44.3 0.0 copy-done.7
  44.3 1.0 %shard_map.129 = bf16[96,4,128]{2,1,0:T(4,128)(2,1)S(1)} custom-call(bf16[96,4,128]{2,1,0:T(4,128)(2,1)S(1)} %bitcast.17, f32[16,2,512]{2,1,0:T(2,128)S(1)} %bitcast.20, f32[16,2,512]{2,1,0:T(2,128)S(1)} %bitcast.21, f32[96,128]{1,0:T(8,128)S(1)} %copy-done.7), custom_call_target="tpu_custom_call" | custom-call | flops 1000000000 | bytes 1000000 | tf_op jit(solution)/shard_map/pallas_call | solution.py:465
  45.3 0.0 copy-start
  45.3 0.0 copy-start.1
  45.3 0.0 copy-start.6
  45.3 0.0 copy-start.8
  45.3 0.0 copy-start.9
  45.4 11.7 %all_to_all.22 = bf16[32,3,4,128]{3,2,1,0:T(4,128)(2,1)S(1)} all-to-all(bf16[32,3,4,128]{3,2,1,0:T(4,128)(2,1)S(1)} %bitcast.18), channel_id=1, replica_groups={{16,160,208,400,336,128,240,416,112,0,448,288,96,64,320,384,192,256,48,..., dimensions={0} | all-to-all | bytes 196608 | tf_op jit(solution)/shard_map/all_to_all | solution.py:431
  57.0 0.0 copy-done.4
  57.0 0.7 shard_map.130
  57.7 12.3 %all_to_all.23 = bf16[16,8,512]{2,1,0:T(8,128)(2,1)S(1)} all-to-all(bf16[16,8,512]{2,1,0:T(8,128)(2,1)S(1)} %bitcast.15), channel_id=1, replica_groups={{0,2,4,6,8,10,12,14,1,3,5,7,9,11,13,15},{16,18,20,22,24,26,28,30,17,19,..., dimensions={0} | all-to-all | bytes 262144 | tf_op jit(solution)/shard_map/all_to_all | solution.py:431
  70.0 0.0 copy-done
  70.0 0.0 copy-done.1
  70.0 0.0 copy-done.6
  70.0 0.0 copy-done.8
  70.0 0.0 copy-done.9
  70.0 2.3 %shard_map.131 = f32[2,1536]{1,0:T(2,128)} custom-call(bf16[128,512]{1,0:T(8,128)(2,1)S(1)} %bitcast.13, s32[24,128]{1,0:T(8,128)S(1)} %copy-done.9, bf16[16,256,128]{2,1,0:T(8,128)(2,1)S(1)} %copy-done, f32[32,128]{1,0:T(8,128)S(1)} %copy-done.8, bf16[8,2,128,128]{3,2,1,0:T(8,128)(2,1)S(1)} %copy-done.1, f32[128,128]{1,0:T(8,128)S(1)} %copy-done.6), custom_call_target="tpu_custom_call" | custom-call | flops 1000000000 | bytes 2000000 | tf_op jit(solution)/shard_map/pallas_call | solution.py:471
Async XLA Ops:
  0.0 25.9 %copy-start.5 = (f32[240,128]{1,0:T(8,128)S(1)}, f32[240,128]{1,0:T(8,128)}, u32[]{:S(2)}) copy-start(f32[240,128]{1,0:T(8,128)} %constant.12.clone.table_ref) | copy-start | bytes 368644
  3.2 41.0 %copy-start.2 = (f32[512,16,2]{0,2,1:T(2,128)S(1)}, f32[512,16,2]{0,2,1:T(2,128)}, u32[]{:S(2)}) copy-start(f32[512,16,2]{0,2,1:T(2,128)} %param.19) | copy-start | bytes 196612
  3.2 41.0 %copy-start.3 = (f32[512,16,2]{0,2,1:T(2,128)S(1)}, f32[512,16,2]{0,2,1:T(2,128)}, u32[]{:S(2)}) copy-start(f32[512,16,2]{0,2,1:T(2,128)} %param.20) | copy-start | bytes 196612
  3.2 41.0 %copy-start.7 = (f32[96,128]{1,0:T(8,128)S(1)}, f32[96,128]{1,0:T(8,128)}, u32[]{:S(2)}) copy-start(f32[96,128]{1,0:T(8,128)} %constant.14.clone.table_ref) | copy-start | bytes 147460
  26.7 30.3 %copy-start.4 = (f32[248,128]{1,0:T(8,128)S(1)}, f32[248,128]{1,0:T(8,128)}, u32[]{:S(2)}) copy-start(f32[248,128]{1,0:T(8,128)} %constant.13.clone.table_ref) | copy-start | bytes 380932
  45.3 24.7 %copy-start = (bf16[16,256,128]{2,1,0:T(8,128)(2,1)S(1)}, bf16[16,256,128]{2,1,0:T(8,128)(2,1)}, u32[]{:S(2)}) copy-start(bf16[16,256,128]{2,1,0:T(8,128)(2,1)} %proj_ref.1) | copy-start | bytes 3145732
  45.3 24.7 %copy-start.1 = (bf16[8,2,128,128]{3,2,1,0:T(8,128)(2,1)S(1)}, bf16[8,2,128,128]{3,2,1,0:T(8,128)(2,1)}, u32[]{:S(2)}) copy-start(bf16[8,2,128,128]{3,2,1,0:T(8,128)(2,1)} %blocks_ref.1) | copy-start | bytes 1572868
  45.3 24.7 %copy-start.6 = (f32[128,128]{1,0:T(8,128)S(1)}, f32[128,128]{1,0:T(8,128)}, u32[]{:S(2)}) copy-start(f32[128,128]{1,0:T(8,128)} %constant.11.clone.table_ref) | copy-start | bytes 196612
  45.3 24.7 %copy-start.8 = (f32[32,128]{1,0:T(8,128)S(1)}, f32[32,128]{1,0:T(8,128)}, u32[]{:S(2)}) copy-start(f32[32,128]{1,0:T(8,128)} %get-tuple-element.10.slots_ref) | copy-start | bytes 49156
  45.3 24.7 %copy-start.9 = (s32[24,128]{1,0:T(8,128)S(1)}, s32[24,128]{1,0:T(8,128)}, u32[]{:S(2)}) copy-start(s32[24,128]{1,0:T(8,128)} %get-tuple-element.9.ints_ref) | copy-start | bytes 36868

commit v3 on v2

--- a/solution.py
+++ b/solution.py
@@ -22,7 +22,6 @@
 F32 = jnp.float32
 BF16 = jnp.bfloat16
 VMEM_LIMIT = 16 * 1024 * 1024
-LIMIT_A = 65536 * 1024 - 960 * 1024
 
 
 def split_table(table):
@@ -44,7 +43,7 @@
     table = np.einsum("jqzoc,hg->jhqogcz", forward, np.eye(2)).reshape(128, 128)
     backward = as_real(theta, True).reshape(16, 2, 32, 2, 2)[list(ORDER_Y)] / 32.0
     table_back = np.einsum("jqzoc,hg->jhqcgoz", backward, np.eye(2)).reshape(128, 128)
-    first = np.zeros((4096, 256), ml_dtypes.bfloat16)
+    first = np.zeros((384, 256), ml_dtypes.bfloat16)
     p = np.arange(256)
     first[p, (p // 32 % 2) * 128 + (p // 64) * NV + p // 4 % 8] = 1.0
     first[256:384, 0:128], first[256:384, 128:256] = split_table(table)
@@ -129,6 +128,10 @@
 
 def slot_picks(slot):
     return jnp.where(iota((SLOTS, SOURCES), 0) == (slot & 127), 1.0, 0.0).astype(BF16)
+
+
+def side_by_side(ref, n):
+    return jnp.concatenate([ref[n], ref[n + 1]], axis=1)
 
 
 def spread_kernel(
@@ -160,9 +163,8 @@
         (anchor_hbm, anchor_ref),
         (anchor_hbm, anchor_vec),
         (pairs_hbm, pairs_vec),
-        (proj_hbm, proj_ref),
-        (tables_hbm.at[0:384], tables_ref),
-    )
+    ) + tuple((proj_hbm.at[n : n + 4], proj_ref.at[n : n + 4]) for n in range(0, TILES, 4))
+    fetched = fetched + ((tables_hbm, tables_ref),)
     copies = [pltpu.make_async_copy(src, dst, sems.at[n]) for n, (src, dst) in enumerate(fetched)]
     for copy in copies:
         copy.start()
@@ -179,9 +181,13 @@
     held = jnp.where(row // 2 == (slot >> 7), charge, 0.0).astype(BF16)
     slots_ref[...] = mm_nt(held, slot_picks(slot))
     picks = layer_picks(anchor_vec[...])
-    copies[5].wait()
-    for t in range(TILES):
-        nodes[2 * t : 2 * t + 2, :] = mm_nt(slots_ref[2 * t : 2 * t + 2, :].astype(BF16), proj_ref[t])
+    first = iota((4, SLOTS), 0) < 2
+    for t in range(0, TILES, 2):
+        if t % 4 == 0:
+            copies[5 + t // 4].wait()
+        mine = slots_ref[2 * t : 2 * t + 4, :]
+        mine = jnp.concatenate([jnp.where(first, mine, 0.0), jnp.where(first, 0.0, mine)], axis=1)
+        nodes[2 * t : 2 * t + 4, :] = mm_nt(mine.astype(BF16), side_by_side(proj_ref, t))
     value = nodes[...]
     layer = iota((32, 128), 1) % 4
     for half in range(2):
@@ -189,7 +195,7 @@
             part = value[:, 128 * half : 128 * half + 128]
             layers[pl.ds(128 * half + b, 32, stride=4), :] = jnp.where(layer == b, part, 0.0)
     high, low = halves(jnp.concatenate([layers[0:128, :], layers[128:256, :]], axis=1))
-    copies[6].wait()
+    copies[9].wait()
     spread = tables_ref[0:256, :]
     patch[...] = mm(high, spread) + mm(low, spread)
     empty = jnp.zeros((8, 128), F32)
@@ -351,13 +357,15 @@
     patch,
     layers,
     nodes,
+    pick,
     near,
     total,
     sem,
 ):
     copy = pltpu.make_async_copy(ints_ref.at[16:24], anchor_ref, sem)
     copy.start()
-    near[...] = jnp.zeros_like(near)
+    slot = as_row(ints_ref[0 : SOURCES // 128, :])
+    pick[...] = slot_picks(slot)
     picks = layer_picks(ints_ref[16:19, 0:TILES])
     tab = halves(table_ref[...])
     phase_high = mm(tab[0], picks).T.astype(BF16)
@@ -367,12 +375,20 @@
     cells[...] = field.astype(BF16).astype(F32)
     copy.wait()
     sign = jnp.where(iota((2, 128), 0) == 0, -1.0, 1.0)
-    for q in range(8):
-        source = slots_ref[pl.ds(anchor_ref[5, q] * 2, 2), :]
-        turn = jnp.concatenate([source[1:2], source[0:1]], axis=0) * sign
-        value = mm_nt(source.astype(BF16), blocks_ref[q, 0]) + mm_nt(turn.astype(BF16), blocks_ref[q, 1])
+    values = []
+    for q in range(0, PAIRS, 2):
+        lines = []
+        for n in (q, q + 1):
+            source = slots_ref[pl.ds(anchor_ref[5, n] * 2, 2), :]
+            turn = jnp.concatenate([source[1:2], source[0:1]], axis=0) * sign
+            lines.append(jnp.concatenate([source, turn], axis=1))
+        blocks = jnp.concatenate([side_by_side(blocks_ref.at[q], 0), side_by_side(blocks_ref.at[q + 1], 0)], axis=0)
+        value = mm_nt(jnp.concatenate(lines, axis=0).astype(BF16), blocks)
+        values.extend((value[0:2, 0:SLOTS], value[2:4, SLOTS:]))
+    near[...] = jnp.zeros_like(near)
+    for q in range(PAIRS):
         target = pl.ds(anchor_ref[4, q] * 2, 2)
-        near[target, :] = near[target, :] + value
+        near[target, :] = near[target, :] + values[q]
     for t in range(TILES):
         odd, starts = place(anchor_ref, t)
         parts = []
@@ -391,12 +407,12 @@
         for b in range(1, 4):
             value = jnp.where(layer == b, layers[pl.ds(128 * half + b, 32, stride=4), :], value)
         nodes[:, 128 * half : 128 * half + 128] = value
-    for t in range(TILES):
-        total[2 * t : 2 * t + 2, :] = mm(nodes[2 * t : 2 * t + 2, :].astype(BF16), proj_ref[t])
+    first = iota((4, SLOTS), 0) < 2
+    for t in range(0, TILES, 2):
+        value = mm(nodes[2 * t : 2 * t + 4, :].astype(BF16), side_by_side(proj_ref, t))
+        total[2 * t : 2 * t + 4, :] = jnp.where(first, value[:, 0:SLOTS], value[:, SLOTS:])
     high, low = halves(total[...] + near[...])
-    slot = as_row(ints_ref[0 : SOURCES // 128, :])
-    pick = slot_picks(slot)
-    value = mm(high, pick) + mm(low, pick)
+    value = mm(high, pick[...]) + mm(low, pick[...])
     value = jnp.where(iota((32, SOURCES), 0) // 2 == (slot >> 7), value, 0.0)
     value = value[0:8] + value[8:16] + value[16:24] + value[24:32]
     value = value + pltpu.roll(value, 4, 0)
@@ -408,20 +424,24 @@
 HB = pl.BlockSpec(memory_space=pltpu.HBM)
 
 
-def call(kernel, outs, in_specs, scratch, flops, moved, limit=VMEM_LIMIT):
+def call(kernel, outs, in_specs, scratch, flops, moved):
     return pl.pallas_call(
         kernel,
-        out_shape=[shape(*out.shape, dtype=out.dtype) for out in outs],
+        out_shape=outs,
         in_specs=in_specs,
         out_specs=[VM] * len(outs),
         scratch_shapes=scratch,
-        compiler_params=pltpu.CompilerParams(vmem_limit_bytes=limit),
+        compiler_params=pltpu.CompilerParams(vmem_limit_bytes=VMEM_LIMIT),
         cost_estimate=pl.CostEstimate(flops=flops, bytes_accessed=moved, transcendentals=0),
     )
 
 
 def shape(*dims, dtype=F32):
     return jax.ShapeDtypeStruct(dims, dtype)
+
+
+def held(*dims, dtype=F32):
+    return pltpu.VMEM(dims, dtype)
 
 
 def swap(cells, axis):
@@ -438,7 +458,7 @@
     block = pltpu.VMEM((384, 128), F32)
     cells, slots, ints = call(
         spread_kernel,
-        [shape(128, CELLS, dtype=BF16), shape(32, SLOTS), shape(24, 128, dtype=jnp.int32)],
+        [held(128, CELLS, dtype=BF16), held(32, SLOTS), held(24, 128, dtype=jnp.int32)],
         [HB] * 6,
         [
             pltpu.VMEM((2, SOURCES), F32),
@@ -452,21 +472,25 @@
             pltpu.VMEM((256, 128), F32),
             pltpu.VMEM((128, 256), F32),
             pltpu.VMEM((256, CELLS), F32),
-            pltpu.SemaphoreType.DMA((7,)),
+            pltpu.SemaphoreType.DMA((10,)),
         ],
         10**9,
         2 * 10**6,
-        LIMIT_A,
-    )(charges, source_slot.reshape(SOURCES // 128, 128), tile_anchor.T, near_pairs.T, projection, first)
+    )(
+        *[
+            pltpu.with_memory_space_constraint(array, pltpu.HBM)
+            for array in (charges, source_slot.reshape(-1, 128), tile_anchor.T, near_pairs.T, projection, first)
+        ]
+    )
     cells = swap(cells, "gy")
-    lines = shape(*LINES, dtype=BF16)
-    lines = call(y_kernel, [lines], [VM] * 2, [block], 10**9, 10**6)(cells, y_table)[0]
+    line_shape = held(*LINES, dtype=BF16)
+    lines = call(y_kernel, [line_shape], [VM] * 2, [block], 10**9, 10**6)(cells, y_table)[0]
     lines = swap(lines, "gx")
-    lines = call(x_kernel, [lines], [VM] * 4, [block] * 2, 10**9, 10**6)(
+    lines = call(x_kernel, [line_shape], [VM] * 4, [block] * 2, 10**9, 10**6)(
         lines, green_real.transpose(1, 2, 0), green_imag.transpose(1, 2, 0), x_tables()
     )[0]
     lines = swap(lines, "gx")
-    cells = call(y_back_kernel, [cells], [VM] * 2, [block] * 2, 10**9, 10**6)(lines, y_back)[0]
+    cells = call(y_back_kernel, [held(128, CELLS, dtype=BF16)], [VM] * 2, [block] * 2, 10**9, 10**6)(lines, y_back)[0]
     cells = swap(cells, "gy")
     return call(
         gather_kernel,
@@ -478,6 +502,7 @@
             pltpu.VMEM((128, 256), F32),
             pltpu.VMEM((256, 128), F32),
             pltpu.VMEM((32, 256), F32),
+            pltpu.VMEM((SLOTS, SOURCES), BF16),
             pltpu.VMEM((32, SLOTS), F32),
             pltpu.VMEM((32, SLOTS), F32),
             pltpu.SemaphoreType.DMA,

time: 72.9 us -> 72 us (0.988)
  no operation moved by 1% of the time
where the time goes in v3:
time: 72 us; the launch traced here: 71.4 us
  blocking collectives  63.9 us (89%)
  Pallas kernels  7.36 us (10%)
    all_to_all x4, blocking collectives, swap(): lax.all_to_all(blocks, axis, 0, 0, axis_index_groups=[list(order)], tiled...  63.9 us
    pallas_call x1, Pallas kernels, body(): call(spread_kernel, [held(128, CELLS, dtype=BF16), held(32, SLOTS), held(...  2.74 us
    pallas_call x1, Pallas kernels, body(): call(gather_kernel, [shape(2, SOURCES)], [VM] * 6, [pltpu.SMEM((8, 128),...  2.09 us

profile of v3, /device:TPU:1, one launch (start us, length us, event | category | flops | bytes accessed | tf_op | source)
XLA Modules:
  0.0 71.4 jit_solution(10774663704443450948)
XLA Ops:
  0.0 2.7 %shard_map.127 = (bf16[128,512]{1,0:T(8,128)(2,1)S(1)}, f32[32,128]{1,0:T(8,128)S(1)}, s32[24,128]{1,0:T(8,128)S(1)}) custom-call(f32[2,1536]{1,0:T(2,128)} %charges_hbm.1, s32[12,128]{1,0:T(8,128)} %bitcast.23, s32[3,16]{1,0:T(4,128)} %bitcast.24, s32[2,8]{1,0:T(2,128)} %bitcast.25, bf16[16,256,128]{2,1,0:T(8,128)(2,1)} %proj_ref.1, ...), custom_call_target="tpu_custom_call" | custom-call | flops 1000000000 | bytes 2000000 | tf_op jit(solution)/shard_map/pallas_call | solution.py:459
  2.7 0.0 copy-start.5
  2.8 22.3 %all_to_all.20 = bf16[16,8,512]{2,1,0:T(8,128)(2,1)S(1)} all-to-all(bf16[16,8,512]{2,1,0:T(8,128)(2,1)S(1)} %bitcast.14), channel_id=1, replica_groups={{0,2,4,6,8,10,12,14,1,3,5,7,9,11,13,15},{16,18,20,22,24,26,28,30,17,19,..., dimensions={0} | all-to-all | bytes 262144 | tf_op jit(solution)/shard_map/all_to_all | solution.py:451
  25.1 0.0 copy-done.5
  25.1 0.8 %shard_map.128 = bf16[96,4,128]{2,1,0:T(4,128)(2,1)S(1)} custom-call(bf16[128,512]{1,0:T(8,128)(2,1)S(1)} %bitcast.15, f32[240,128]{1,0:T(8,128)S(1)} %copy-done.5), custom_call_target="tpu_custom_call" | custom-call | flops 1000000000 | bytes 1000000 | tf_op jit(solution)/shard_map/pallas_call | solution.py:487
  25.9 0.0 copy-start.2
  25.9 0.0 copy-start.3
  25.9 0.0 copy-start.7
  25.9 17.6 %all_to_all.21 = bf16[32,3,4,128]{3,2,1,0:T(4,128)(2,1)S(1)} all-to-all(bf16[32,3,4,128]{3,2,1,0:T(4,128)(2,1)S(1)} %bitcast.17), channel_id=1, replica_groups={{16,160,208,400,336,128,240,416,112,0,448,288,96,64,320,384,192,256,48,..., dimensions={0} | all-to-all | bytes 196608 | tf_op jit(solution)/shard_map/all_to_all | solution.py:451
  43.6 0.0 copy-done.2
  43.6 0.0 copy-done.3
  43.6 0.0 copy-done.7
  43.6 1.0 %shard_map.129 = bf16[96,4,128]{2,1,0:T(4,128)(2,1)S(1)} custom-call(bf16[96,4,128]{2,1,0:T(4,128)(2,1)S(1)} %bitcast.18, f32[16,2,512]{2,1,0:T(2,128)S(1)} %bitcast.21, f32[16,2,512]{2,1,0:T(2,128)S(1)} %bitcast.22, f32[96,128]{1,0:T(8,128)S(1)} %copy-done.7), custom_call_target="tpu_custom_call" | custom-call | flops 1000000000 | bytes 1000000 | tf_op jit(solution)/shard_map/pallas_call | solution.py:489
  44.6 0.0 copy-start.4
  44.6 11.7 %all_to_all.22 = bf16[32,3,4,128]{3,2,1,0:T(4,128)(2,1)S(1)} all-to-all(bf16[32,3,4,128]{3,2,1,0:T(4,128)(2,1)S(1)} %bitcast.19), channel_id=1, replica_groups={{16,160,208,400,336,128,240,416,112,0,448,288,96,64,320,384,192,256,48,..., dimensions={0} | all-to-all | bytes 196608 | tf_op jit(solution)/shard_map/all_to_all | solution.py:451
  56.3 0.0 copy-done.4
  56.3 0.0 copy-start
  56.3 0.0 copy-start.1
  56.3 0.7 shard_map.130
  57.0 0.0 copy-start.6
  57.0 12.3 %all_to_all.23 = bf16[16,8,512]{2,1,0:T(8,128)(2,1)S(1)} all-to-all(bf16[16,8,512]{2,1,0:T(8,128)(2,1)S(1)} %bitcast.16), channel_id=1, replica_groups={{0,2,4,6,8,10,12,14,1,3,5,7,9,11,13,15},{16,18,20,22,24,26,28,30,17,19,..., dimensions={0} | all-to-all | bytes 262144 | tf_op jit(solution)/shard_map/all_to_all | solution.py:451
  69.3 0.0 copy-done
  69.3 0.0 copy-done.1
  69.3 0.0 copy-done.6
  69.3 2.1 %shard_map.131 = f32[2,1536]{1,0:T(2,128)} custom-call(bf16[128,512]{1,0:T(8,128)(2,1)S(1)} %bitcast.13, s32[24,128]{1,0:T(8,128)S(1)} %get-tuple-element.9.ints_ref, bf16[16,256,128]{2,1,0:T(8,128)(2,1)S(1)} %copy-done, f32[32,128]{1,0:T(8,128)S(1)} %get-tuple-element.10.slots_ref, bf16[8,2,128,128]{3,2,1,0:T(8,128)(2,1)S(1)} %copy-done.1, ...), custom_call_target="tpu_custom_call" | custom-call | flops 1000000000 | bytes 2000000 | tf_op jit(solution)/shard_map/pallas_call | solution.py:495
Async XLA Ops:
  2.7 22.3 %copy-start.5 = (f32[240,128]{1,0:T(8,128)S(1)}, f32[240,128]{1,0:T(8,128)}, u32[]{:S(2)}) copy-start(f32[240,128]{1,0:T(8,128)} %constant.12.clone.table_ref) | copy-start | bytes 368644
  25.9 17.7 %copy-start.2 = (f32[512,16,2]{0,2,1:T(2,128)S(1)}, f32[512,16,2]{0,2,1:T(2,128)}, u32[]{:S(2)}) copy-start(f32[512,16,2]{0,2,1:T(2,128)} %param.19) | copy-start | bytes 196612
  25.9 17.6 %copy-start.3 = (f32[512,16,2]{0,2,1:T(2,128)S(1)}, f32[512,16,2]{0,2,1:T(2,128)}, u32[]{:S(2)}) copy-start(f32[512,16,2]{0,2,1:T(2,128)} %param.20) | copy-start | bytes 196612
  25.9 17.6 %copy-start.7 = (f32[96,128]{1,0:T(8,128)S(1)}, f32[96,128]{1,0:T(8,128)}, u32[]{:S(2)}) copy-start(f32[96,128]{1,0:T(8,128)} %constant.14.clone.table_ref) | copy-start | bytes 147460
  44.6 11.7 %copy-start.4 = (f32[248,128]{1,0:T(8,128)S(1)}, f32[248,128]{1,0:T(8,128)}, u32[]{:S(2)}) copy-start(f32[248,128]{1,0:T(8,128)} %constant.13.clone.table_ref) | copy-start | bytes 380932
  56.3 13.0 %copy-start = (bf16[16,256,128]{2,1,0:T(8,128)(2,1)S(1)}, bf16[16,256,128]{2,1,0:T(8,128)(2,1)}, u32[]{:S(2)}) copy-start(bf16[16,256,128]{2,1,0:T(8,128)(2,1)} %proj_ref.1) | copy-start | bytes 3145732
  56.3 13.0 %copy-start.1 = (bf16[8,2,128,128]{3,2,1,0:T(8,128)(2,1)S(1)}, bf16[8,2,128,128]{3,2,1,0:T(8,128)(2,1)}, u32[]{:S(2)}) copy-start(bf16[8,2,128,128]{3,2,1,0:T(8,128)(2,1)} %blocks_ref.1) | copy-start | bytes 1572868
  57.0 12.3 %copy-start.6 = (f32[128,128]{1,0:T(8,128)S(1)}, f32[128,128]{1,0:T(8,128)}, u32[]{:S(2)}) copy-start(f32[128,128]{1,0:T(8,128)} %constant.11.clone.table_ref) | copy-start | bytes 196612

commit v4 on v3

--- a/solution.py
+++ b/solution.py
@@ -15,7 +15,7 @@
 SOURCES = 1536
 NU = 12
 LINES = (96, 4, 128)
-ORDER_X = (1, 10, 13, 25, 21, 8, 15, 26, 7, 0, 28, 18, 6, 4, 20, 24, 12, 16, 3, 2, 31, 14, 23, 29, 5, 11, 17, 27, 30, 22, 9, 19)
+ORDER_X = (1, 10, 19, 14, 6, 7, 15, 13, 18, 20, 24, 0, 11, 31, 5, 30, 4, 3, 26, 2, 9, 21, 22, 29, 23, 28, 8, 27, 12, 17, 16, 25)
 ORDER_Y = tuple(2 * z + x for x in range(2) for z in range(8))
 NV = 40
 CELLS = 512
@@ -91,6 +91,20 @@
 def halves(value):
     high = value.astype(BF16)
     return high, (value - high.astype(F32)).astype(BF16)
+
+
+def thrice(value, axis):
+    high, low = halves(value)
+    return jnp.concatenate([high, low, high], axis=axis)
+
+
+def thrice_other(value, axis):
+    high, low = halves(value)
+    return jnp.concatenate([high, high, low], axis=axis)
+
+
+def twice(value, axis):
+    return jnp.concatenate([value, value], axis=axis)
 
 
 def iota(shape, axis):
@@ -163,7 +177,7 @@
         (anchor_hbm, anchor_ref),
         (anchor_hbm, anchor_vec),
         (pairs_hbm, pairs_vec),
-    ) + tuple((proj_hbm.at[n : n + 4], proj_ref.at[n : n + 4]) for n in range(0, TILES, 4))
+    ) + tuple((proj_hbm.at[n : n + 8], proj_ref.at[n : n + 8]) for n in range(0, TILES, 8))
     fetched = fetched + ((tables_hbm, tables_ref),)
     copies = [pltpu.make_async_copy(src, dst, sems.at[n]) for n, (src, dst) in enumerate(fetched)]
     for copy in copies:
@@ -183,8 +197,8 @@
     picks = layer_picks(anchor_vec[...])
     first = iota((4, SLOTS), 0) < 2
     for t in range(0, TILES, 2):
-        if t % 4 == 0:
-            copies[5 + t // 4].wait()
+        if t % 8 == 0:
+            copies[5 + t // 8].wait()
         mine = slots_ref[2 * t : 2 * t + 4, :]
         mine = jnp.concatenate([jnp.where(first, mine, 0.0), jnp.where(first, 0.0, mine)], axis=1)
         nodes[2 * t : 2 * t + 4, :] = mm_nt(mine.astype(BF16), side_by_side(proj_ref, t))
@@ -195,7 +209,7 @@
             part = value[:, 128 * half : 128 * half + 128]
             layers[pl.ds(128 * half + b, 32, stride=4), :] = jnp.where(layer == b, part, 0.0)
     high, low = halves(jnp.concatenate([layers[0:128, :], layers[128:256, :]], axis=1))
-    copies[9].wait()
+    copies[7].wait()
     spread = tables_ref[0:256, :]
     patch[...] = mm(high, spread) + mm(low, spread)
     empty = jnp.zeros((8, 128), F32)
@@ -221,15 +235,17 @@
     cos, sin = table_ref[0:NV, :], table_ref[NV : 2 * NV, :]
     table = table_ref[2 * NV : 2 * NV + 128, :]
     high, low = halves(jnp.concatenate([table, turned(table)], axis=1))
-    both = mm(data, high) + mm(data, low)
-    rows = halves(table_ref[2 * NV + 128 : 2 * NV + 160, 0 : 2 * NV])
-    for u in range(NU):
-        plain = both[NV * u : NV * (u + 1), 0:128]
-        turn = both[NV * u : NV * (u + 1), 128:256]
-        lines = jnp.concatenate([plain * cos + turn * sin, turn * cos - plain * sin], axis=0)
-        high, low = halves(lines)
-        out = mm(rows[0], high) + mm(rows[0], low) + mm(rows[1], high)
-        hold[pl.ds(u, 32, stride=NU), :] = out
+    both = mm(twice(data, 1), jnp.concatenate([high, low], axis=0))
+    rows = thrice_other(table_ref[2 * NV + 128 : 2 * NV + 160, 0 : 2 * NV], 1)
+    for u in range(0, NU, 2):
+        lines = []
+        for n in (u, u + 1):
+            plain = both[NV * n : NV * (n + 1), 0:128]
+            turn = both[NV * n : NV * (n + 1), 128:256]
+            lines.append(jnp.concatenate([plain * cos + turn * sin, turn * cos - plain * sin], axis=0))
+        out = mm(rows, thrice(jnp.concatenate(lines, axis=1), 0))
+        hold[pl.ds(u, 32, stride=NU), :] = out[:, 0:128]
+        hold[pl.ds(u + 1, 32, stride=NU), :] = out[:, 128:256]
     out_ref[...] = hold[...].reshape(LINES).astype(BF16)
 
 
@@ -266,12 +282,12 @@
     four = jnp.concatenate(
         [jnp.concatenate([plain, turn], axis=1), jnp.concatenate([turn, -plain], axis=1)], axis=0
     ).astype(BF16)
-    return mm(rows[0], four) + mm(rows[1], four)
+    return mm(rows, twice(four, 0))
 
 
 def x_kernel(in_ref, real_ref, imag_ref, table_ref, out_ref, hold, hold_turned):
-    into = halves(table_ref[0:32, 0:64])
-    back = halves(table_ref[32:64, 0:64])
+    into = jnp.concatenate(halves(table_ref[0:32, 0:64]), axis=1)
+    back = thrice_other(table_ref[32:64, 0:64], 1)
     angles = table_ref[64:96, :]
     second = iota((32, 128), 1) >= 64
 
@@ -310,12 +326,14 @@
         plain, turn = plain * real[rows] - turn * imag[rows], turn * real[rows] + plain * imag[rows]
         lines[n] = rotated((crossed(plain), crossed(turn)), cos, -sin)
     classes = short_dft(lines, -1)
-    for u in range(NU):
-        cos, sin = step(u)
-        value = rotated(classes[(u - 2) % 8], cos, -sin)
-        high, low = halves(jnp.concatenate(value, axis=0))
-        out = mm(back[0], high) + mm(back[0], low) + mm(back[1], high)
-        hold[pl.ds(u, 32, stride=NU), :] = out
+    for u in range(0, NU, 2):
+        values = []
+        for n in (u, u + 1):
+            cos, sin = step(n)
+            values.append(jnp.concatenate(rotated(classes[(n - 2) % 8], cos, -sin), axis=0))
+        out = mm(back, thrice(jnp.concatenate(values, axis=1), 0))
+        hold[pl.ds(u, 32, stride=NU), :] = out[:, 0:128]
+        hold[pl.ds(u + 1, 32, stride=NU), :] = out[:, 128:256]
     out_ref[...] = hold[...].reshape(LINES).astype(BF16)
 
 
@@ -324,8 +342,8 @@
     hold[...] = data
     hold_turned[...] = turned(data)
     cos, sin = table_ref[0:NV, :], table_ref[NV : 2 * NV, :]
-    tab = halves(table_ref[2 * NV : 2 * NV + 128, :])
-    rows = halves(table_ref[2 * NV + 128 : 3 * NV + 128, 0:64])
+    tab = thrice_other(table_ref[2 * NV : 2 * NV + 128, :], 1)
+    rows = jnp.concatenate(halves(table_ref[2 * NV + 128 : 3 * NV + 128, 0:64]), axis=1)
     lines = []
     for u in range(NU):
         plain = hold[pl.ds(u, 32, stride=NU), :]
@@ -333,8 +351,7 @@
         both = line_pair(rows, plain, turn)
         lines.append(both[:, 0:128] * cos - both[:, 128:256] * sin)
     lines.append(jnp.zeros((CELLS - NU * NV, 128), F32))
-    high, low = halves(jnp.concatenate(lines, axis=0))
-    out = mm_nt(tab[0], high) + mm_nt(tab[0], low) + mm_nt(tab[1], high)
+    out = mm_nt(tab, thrice(jnp.concatenate(lines, axis=0), 1))
     out_ref[...] = out.astype(BF16)
 
 
@@ -368,10 +385,8 @@
     pick[...] = slot_picks(slot)
     picks = layer_picks(ints_ref[16:19, 0:TILES])
     tab = halves(table_ref[...])
-    phase_high = mm(tab[0], picks).T.astype(BF16)
-    phase_low = mm(tab[1], picks).T.astype(BF16)
-    data = in_ref[...]
-    field = mm(phase_high, data) + mm(phase_low, data)
+    phase = mm(jnp.concatenate(tab, axis=0), picks).T.astype(BF16)
+    field = mm(phase, twice(in_ref[...], 0))
     cells[...] = field.astype(BF16).astype(F32)
     copy.wait()
     sign = jnp.where(iota((2, 128), 0) == 0, -1.0, 1.0)
@@ -411,8 +426,7 @@
     for t in range(0, TILES, 2):
         value = mm(nodes[2 * t : 2 * t + 4, :].astype(BF16), side_by_side(proj_ref, t))
         total[2 * t : 2 * t + 4, :] = jnp.where(first, value[:, 0:SLOTS], value[:, SLOTS:])
-    high, low = halves(total[...] + near[...])
-    value = mm(high, pick[...]) + mm(low, pick[...])
+    value = mm(jnp.concatenate(halves(total[...] + near[...]), axis=1), twice(pick[...], 0))
     value = jnp.where(iota((32, SOURCES), 0) // 2 == (slot >> 7), value, 0.0)
     value = value[0:8] + value[8:16] + value[16:24] + value[24:32]
     value = value + pltpu.roll(value, 4, 0)
@@ -472,7 +486,7 @@
             pltpu.VMEM((256, 128), F32),
             pltpu.VMEM((128, 256), F32),
             pltpu.VMEM((256, CELLS), F32),
-            pltpu.SemaphoreType.DMA((10,)),
+            pltpu.SemaphoreType.DMA((8,)),
         ],
         10**9,
         2 * 10**6,

time: 72 us -> 71 us (0.986)
  no operation moved by 1% of the time
where the time goes in v4:
time: 71 us; the launch traced here: 70.5 us
  blocking collectives  63.7 us (90%)
  Pallas kernels  6.65 us (9%)
    all_to_all x4, blocking collectives, swap(): lax.all_to_all(blocks, axis, 0, 0, axis_index_groups=[list(order)], tiled...  63.7 us
    pallas_call x1, Pallas kernels, body(): call(spread_kernel, [held(128, CELLS, dtype=BF16), held(32, SLOTS), held(...  2.49 us
    pallas_call x1, Pallas kernels, body(): call(gather_kernel, [shape(2, SOURCES)], [VM] * 6, [pltpu.SMEM((8, 128),...  2 us

profile of v4, /device:TPU:1, one launch (start us, length us, event | category | flops | bytes accessed | tf_op | source)
XLA Modules:
  0.0 70.5 jit_solution(10067779299468641108)
XLA Ops:
  0.0 2.5 %shard_map.127 = (bf16[128,512]{1,0:T(8,128)(2,1)S(1)}, f32[32,128]{1,0:T(8,128)S(1)}, s32[24,128]{1,0:T(8,128)S(1)}) custom-call(f32[2,1536]{1,0:T(2,128)} %charges_hbm.1, s32[12,128]{1,0:T(8,128)} %bitcast.23, s32[3,16]{1,0:T(4,128)} %bitcast.24, s32[2,8]{1,0:T(2,128)} %bitcast.25, bf16[16,256,128]{2,1,0:T(8,128)(2,1)} %proj_ref.1, ...), custom_call_target="tpu_custom_call" | custom-call | flops 1000000000 | bytes 2000000 | tf_op jit(solution)/shard_map/pallas_call | solution.py:473
  2.5 0.0 copy-start.5
  2.5 22.3 %all_to_all.20 = bf16[16,8,512]{2,1,0:T(8,128)(2,1)S(1)} all-to-all(bf16[16,8,512]{2,1,0:T(8,128)(2,1)S(1)} %bitcast.14), channel_id=1, replica_groups={{0,2,4,6,8,10,12,14,1,3,5,7,9,11,13,15},{16,18,20,22,24,26,28,30,17,19,..., dimensions={0} | all-to-all | bytes 262144 | tf_op jit(solution)/shard_map/all_to_all | solution.py:465
  24.8 0.0 copy-done.5
  24.8 0.6 shard_map.128
  25.4 0.0 copy-start.2
  25.4 0.0 copy-start.3
  25.4 0.0 copy-start.7
  25.4 17.4 %all_to_all.21 = bf16[32,3,4,128]{3,2,1,0:T(4,128)(2,1)S(1)} all-to-all(bf16[32,3,4,128]{3,2,1,0:T(4,128)(2,1)S(1)} %bitcast.17), channel_id=1, replica_groups={{16,160,304,224,96,112,240,208,288,320,384,0,176,496,80,480,64,48,416,3..., dimensions={0} | all-to-all | bytes 196608 | tf_op jit(solution)/shard_map/all_to_all | solution.py:465
  42.8 0.0 copy-done.2
  42.8 0.0 copy-done.3
  42.8 0.0 copy-done.7
  42.8 1.0 %shard_map.129 = bf16[96,4,128]{2,1,0:T(4,128)(2,1)S(1)} custom-call(bf16[96,4,128]{2,1,0:T(4,128)(2,1)S(1)} %bitcast.18, f32[16,2,512]{2,1,0:T(2,128)S(1)} %bitcast.21, f32[16,2,512]{2,1,0:T(2,128)S(1)} %bitcast.22, f32[96,128]{1,0:T(8,128)S(1)} %copy-done.7), custom_call_target="tpu_custom_call" | custom-call | flops 1000000000 | bytes 1000000 | tf_op jit(solution)/shard_map/pallas_call | solution.py:503
  43.8 0.0 copy-start.4
  43.9 11.7 %all_to_all.22 = bf16[32,3,4,128]{3,2,1,0:T(4,128)(2,1)S(1)} all-to-all(bf16[32,3,4,128]{3,2,1,0:T(4,128)(2,1)S(1)} %bitcast.19), channel_id=1, replica_groups={{16,160,304,224,96,112,240,208,288,320,384,0,176,496,80,480,64,48,416,3..., dimensions={0} | all-to-all | bytes 196608 | tf_op jit(solution)/shard_map/all_to_all | solution.py:465
  55.5 0.0 copy-done.4
  55.5 0.0 copy-start
  55.5 0.0 copy-start.1
  55.5 0.6 shard_map.130
  56.2 0.0 copy-start.6
  56.2 12.3 %all_to_all.23 = bf16[16,8,512]{2,1,0:T(8,128)(2,1)S(1)} all-to-all(bf16[16,8,512]{2,1,0:T(8,128)(2,1)S(1)} %bitcast.16), channel_id=1, replica_groups={{0,2,4,6,8,10,12,14,1,3,5,7,9,11,13,15},{16,18,20,22,24,26,28,30,17,19,..., dimensions={0} | all-to-all | bytes 262144 | tf_op jit(solution)/shard_map/all_to_all | solution.py:465
  68.5 0.0 copy-done
  68.5 0.0 copy-done.1
  68.5 0.0 copy-done.6
  68.5 2.0 %shard_map.131 = f32[2,1536]{1,0:T(2,128)} custom-call(bf16[128,512]{1,0:T(8,128)(2,1)S(1)} %bitcast.13, s32[24,128]{1,0:T(8,128)S(1)} %get-tuple-element.9.ints_ref, bf16[16,256,128]{2,1,0:T(8,128)(2,1)S(1)} %copy-done, f32[32,128]{1,0:T(8,128)S(1)} %get-tuple-element.10.slots_ref, bf16[8,2,128,128]{3,2,1,0:T(8,128)(2,1)S(1)} %copy-done.1, ...), custom_call_target="tpu_custom_call" | custom-call | flops 1000000000 | bytes 2000000 | tf_op jit(solution)/shard_map/pallas_call | solution.py:509
Async XLA Ops:
  2.5 22.3 %copy-start.5 = (f32[240,128]{1,0:T(8,128)S(1)}, f32[240,128]{1,0:T(8,128)}, u32[]{:S(2)}) copy-start(f32[240,128]{1,0:T(8,128)} %constant.12.clone.table_ref) | copy-start | bytes 368644
  25.4 17.5 %copy-start.2 = (f32[512,16,2]{0,2,1:T(2,128)S(1)}, f32[512,16,2]{0,2,1:T(2,128)}, u32[]{:S(2)}) copy-start(f32[512,16,2]{0,2,1:T(2,128)} %param.19) | copy-start | bytes 196612
  25.4 17.5 %copy-start.3 = (f32[512,16,2]{0,2,1:T(2,128)S(1)}, f32[512,16,2]{0,2,1:T(2,128)}, u32[]{:S(2)}) copy-start(f32[512,16,2]{0,2,1:T(2,128)} %param.20) | copy-start | bytes 196612
  25.4 17.4 %copy-start.7 = (f32[96,128]{1,0:T(8,128)S(1)}, f32[96,128]{1,0:T(8,128)}, u32[]{:S(2)}) copy-start(f32[96,128]{1,0:T(8,128)} %constant.14.clone.table_ref) | copy-start | bytes 147460
  43.8 11.7 %copy-start.4 = (f32[248,128]{1,0:T(8,128)S(1)}, f32[248,128]{1,0:T(8,128)}, u32[]{:S(2)}) copy-start(f32[248,128]{1,0:T(8,128)} %constant.13.clone.table_ref) | copy-start | bytes 380932
  55.5 13.0 %copy-start = (bf16[16,256,128]{2,1,0:T(8,128)(2,1)S(1)}, bf16[16,256,128]{2,1,0:T(8,128)(2,1)}, u32[]{:S(2)}) copy-start(bf16[16,256,128]{2,1,0:T(8,128)(2,1)} %proj_ref.1) | copy-start | bytes 3145732
  55.5 13.0 %copy-start.1 = (bf16[8,2,128,128]{3,2,1,0:T(8,128)(2,1)S(1)}, bf16[8,2,128,128]{3,2,1,0:T(8,128)(2,1)}, u32[]{:S(2)}) copy-start(bf16[8,2,128,128]{3,2,1,0:T(8,128)(2,1)} %blocks_ref.1) | copy-start | bytes 1572868
  56.2 12.3 %copy-start.6 = (f32[128,128]{1,0:T(8,128)S(1)}, f32[128,128]{1,0:T(8,128)}, u32[]{:S(2)}) copy-start(f32[128,128]{1,0:T(8,128)} %constant.11.clone.table_ref) | copy-start | bytes 196612

commit v5 on v4

--- a/solution.py
+++ b/solution.py
@@ -15,7 +15,8 @@
 SOURCES = 1536
 NU = 12
 LINES = (96, 4, 128)
-ORDER_X = (1, 10, 19, 14, 6, 7, 15, 13, 18, 20, 24, 0, 11, 31, 5, 30, 4, 3, 26, 2, 9, 21, 22, 29, 23, 28, 8, 27, 12, 17, 16, 25)
+ROWS = 384
+ORDER_X = (24, 27, 4, 12, 25, 10, 26, 19, 28, 1, 11, 6, 17, 14, 23, 16, 13, 20, 0, 5, 30, 8, 2, 21, 31, 29, 3, 22, 7, 15, 9, 18)
 ORDER_Y = tuple(2 * z + x for x in range(2) for z in range(8))
 NV = 40
 CELLS = 512
@@ -246,7 +247,7 @@
         out = mm(rows, thrice(jnp.concatenate(lines, axis=1), 0))
         hold[pl.ds(u, 32, stride=NU), :] = out[:, 0:128]
         hold[pl.ds(u + 1, 32, stride=NU), :] = out[:, 128:256]
-    out_ref[...] = hold[...].reshape(LINES).astype(BF16)
+    out_ref[...] = hold[0:ROWS, :].reshape(LINES).astype(BF16)
 
 
 def rotated(value, cos, sin):
@@ -300,9 +301,9 @@
         n = n + 2 * NU
         return jnp.where(second, angles[:, n : n + 1], 1.0), jnp.where(second, angles[:, n + 8 : n + 9], 0.0)
 
-    data = in_ref[...].astype(F32).reshape(384, 128)
-    hold[...] = data
-    hold_turned[...] = turned(data)
+    data = in_ref[...].astype(F32).reshape(ROWS, 128)
+    hold[0:ROWS, :] = data
+    hold_turned[0:ROWS, :] = turned(data)
     classes = [None] * 8
     for u in range(NU):
         plain = hold[pl.ds(u, 32, stride=NU), :]
@@ -334,13 +335,13 @@
         out = mm(back, thrice(jnp.concatenate(values, axis=1), 0))
         hold[pl.ds(u, 32, stride=NU), :] = out[:, 0:128]
         hold[pl.ds(u + 1, 32, stride=NU), :] = out[:, 128:256]
-    out_ref[...] = hold[...].reshape(LINES).astype(BF16)
+    out_ref[...] = hold[0:ROWS, :].reshape(LINES).astype(BF16)
 
 
 def y_back_kernel(in_ref, table_ref, out_ref, hold, hold_turned):
-    data = in_ref[...].astype(F32).reshape(384, 128)
-    hold[...] = data
-    hold_turned[...] = turned(data)
+    data = in_ref[...].astype(F32).reshape(ROWS, 128)
+    hold[0:ROWS, :] = data
+    hold_turned[0:ROWS, :] = turned(data)
     cos, sin = table_ref[0:NV, :], table_ref[NV : 2 * NV, :]
     tab = thrice_other(table_ref[2 * NV : 2 * NV + 128, :], 1)
     rows = jnp.concatenate(halves(table_ref[2 * NV + 128 : 3 * NV + 128, 0:64]), axis=1)
@@ -469,7 +470,7 @@
 def body(charges, source_slot, tile_anchor, projection, near_pairs, near_blocks, green_real, green_imag):
     first, z_back = z_tables()
     y_table, y_back = y_tables()
-    block = pltpu.VMEM((384, 128), F32)
+    block = pltpu.VMEM((ROWS + 16, 128), F32)
     cells, slots, ints = call(
         spread_kernel,
         [held(128, CELLS, dtype=BF16), held(32, SLOTS), held(24, 128, dtype=jnp.int32)],
@@ -483,7 +484,7 @@
             pltpu.VMEM((TILES, 256, SLOTS), BF16),
             pltpu.VMEM((384, 256), BF16),
             pltpu.VMEM((32, 256), F32),
-            pltpu.VMEM((256, 128), F32),
+            pltpu.VMEM((264, 128), F32),
             pltpu.VMEM((128, 256), F32),
             pltpu.VMEM((256, CELLS), F32),
             pltpu.SemaphoreType.DMA((8,)),
@@ -514,7 +515,7 @@
             pltpu.SMEM((8, 128), jnp.int32),
             pltpu.VMEM((256, CELLS), F32),
             pltpu.VMEM((128, 256), F32),
-            pltpu.VMEM((256, 128), F32),
+            pltpu.VMEM((264, 128), F32),
             pltpu.VMEM((32, 256), F32),
             pltpu.VMEM((SLOTS, SOURCES), BF16),
             pltpu.VMEM((32, SLOTS), F32),

time: 71 us -> 68.1 us (0.959)
  blocking collectives: 63.7 us -> 60.5 us
    all_to_all x4, blocking collectives: 63.7 us -> 60.5 us  [swap(): lax.all_to_all(blocks, axis, 0, 0, axis_index_groups=[list(order)], tiled...]
where the time goes in v5:
time: 68.1 us; the launch traced here: 67.3 us
  blocking collectives  60.5 us (89%)
  Pallas kernels  6.64 us (10%)
    all_to_all x4, blocking collectives, swap(): lax.all_to_all(blocks, axis, 0, 0, axis_index_groups=[list(order)], tiled...  60.5 us
    pallas_call x1, Pallas kernels, body(): call(spread_kernel, [held(128, CELLS, dtype=BF16), held(32, SLOTS), held(...  2.49 us
    pallas_call x1, Pallas kernels, body(): call(gather_kernel, [shape(2, SOURCES)], [VM] * 6, [pltpu.SMEM((8, 128),...  1.99 us

profile of v5, /device:TPU:1, one launch (start us, length us, event | category | flops | bytes accessed | tf_op | source)
XLA Modules:
  0.0 67.3 jit_solution(12616725750017864065)
XLA Ops:
  0.0 2.5 %shard_map.127 = (bf16[128,512]{1,0:T(8,128)(2,1)S(1)}, f32[32,128]{1,0:T(8,128)S(1)}, s32[24,128]{1,0:T(8,128)S(1)}) custom-call(f32[2,1536]{1,0:T(2,128)} %charges_hbm.1, s32[12,128]{1,0:T(8,128)} %bitcast.23, s32[3,16]{1,0:T(4,128)} %bitcast.24, s32[2,8]{1,0:T(2,128)} %bitcast.25, bf16[16,256,128]{2,1,0:T(8,128)(2,1)} %proj_ref.1, ...), custom_call_target="tpu_custom_call" | custom-call | flops 1000000000 | bytes 2000000 | tf_op jit(solution)/shard_map/pallas_call | solution.py:474
  2.5 0.0 copy-start.5
  2.5 22.3 %all_to_all.20 = bf16[16,8,512]{2,1,0:T(8,128)(2,1)S(1)} all-to-all(bf16[16,8,512]{2,1,0:T(8,128)(2,1)S(1)} %bitcast.14), channel_id=1, replica_groups={{0,2,4,6,8,10,12,14,1,3,5,7,9,11,13,15},{16,18,20,22,24,26,28,30,17,19,..., dimensions={0} | all-to-all | bytes 262144 | tf_op jit(solution)/shard_map/all_to_all | solution.py:466
  24.8 0.0 copy-done.5
  24.8 0.6 shard_map.128
  25.4 0.0 copy-start.2
  25.4 0.0 copy-start.3
  25.4 0.0 copy-start.7
  25.4 14.3 %all_to_all.21 = bf16[32,3,4,128]{3,2,1,0:T(4,128)(2,1)S(1)} all-to-all(bf16[32,3,4,128]{3,2,1,0:T(4,128)(2,1)S(1)} %bitcast.17), channel_id=1, replica_groups={{384,432,64,192,400,160,416,304,448,16,176,96,272,224,368,256,208,320,0..., dimensions={0} | all-to-all | bytes 196608 | tf_op jit(solution)/shard_map/all_to_all | solution.py:466
  39.7 0.0 copy-done.2
  39.7 0.0 copy-done.3
  39.7 0.0 copy-done.7
  39.7 1.0 %shard_map.129 = bf16[96,4,128]{2,1,0:T(4,128)(2,1)S(1)} custom-call(bf16[96,4,128]{2,1,0:T(4,128)(2,1)S(1)} %bitcast.18, f32[16,2,512]{2,1,0:T(2,128)S(1)} %bitcast.21, f32[16,2,512]{2,1,0:T(2,128)S(1)} %bitcast.22, f32[96,128]{1,0:T(8,128)S(1)} %copy-done.7), custom_call_target="tpu_custom_call" | custom-call | flops 1000000000 | bytes 1000000 | tf_op jit(solution)/shard_map/pallas_call | solution.py:504
  40.7 0.0 copy-start.4
  40.7 12.0 %all_to_all.22 = bf16[32,3,4,128]{3,2,1,0:T(4,128)(2,1)S(1)} all-to-all(bf16[32,3,4,128]{3,2,1,0:T(4,128)(2,1)S(1)} %bitcast.19), channel_id=1, replica_groups={{384,432,64,192,400,160,416,304,448,16,176,96,272,224,368,256,208,320,0..., dimensions={0} | all-to-all | bytes 196608 | tf_op jit(solution)/shard_map/all_to_all | solution.py:466
  52.7 0.0 copy-done.4
  52.7 0.0 copy-start
  52.7 0.0 copy-start.1
  52.7 0.6 shard_map.130
  53.3 0.0 copy-start.6
  53.3 12.0 %all_to_all.23 = bf16[16,8,512]{2,1,0:T(8,128)(2,1)S(1)} all-to-all(bf16[16,8,512]{2,1,0:T(8,128)(2,1)S(1)} %bitcast.16), channel_id=1, replica_groups={{0,2,4,6,8,10,12,14,1,3,5,7,9,11,13,15},{16,18,20,22,24,26,28,30,17,19,..., dimensions={0} | all-to-all | bytes 262144 | tf_op jit(solution)/shard_map/all_to_all | solution.py:466
  65.3 0.0 copy-done
  65.3 0.0 copy-done.1
  65.3 0.0 copy-done.6
  65.3 2.0 %shard_map.131 = f32[2,1536]{1,0:T(2,128)} custom-call(bf16[128,512]{1,0:T(8,128)(2,1)S(1)} %bitcast.13, s32[24,128]{1,0:T(8,128)S(1)} %get-tuple-element.9.ints_ref, bf16[16,256,128]{2,1,0:T(8,128)(2,1)S(1)} %copy-done, f32[32,128]{1,0:T(8,128)S(1)} %get-tuple-element.10.slots_ref, bf16[8,2,128,128]{3,2,1,0:T(8,128)(2,1)S(1)} %copy-done.1, ...), custom_call_target="tpu_custom_call" | custom-call | flops 1000000000 | bytes 2000000 | tf_op jit(solution)/shard_map/pallas_call | solution.py:510
Async XLA Ops:
  2.5 22.3 %copy-start.5 = (f32[240,128]{1,0:T(8,128)S(1)}, f32[240,128]{1,0:T(8,128)}, u32[]{:S(2)}) copy-start(f32[240,128]{1,0:T(8,128)} %constant.12.clone.table_ref) | copy-start | bytes 368644
  25.4 14.3 %copy-start.2 = (f32[512,16,2]{0,2,1:T(2,128)S(1)}, f32[512,16,2]{0,2,1:T(2,128)}, u32[]{:S(2)}) copy-start(f32[512,16,2]{0,2,1:T(2,128)} %param.19) | copy-start | bytes 196612
  25.4 14.3 %copy-start.3 = (f32[512,16,2]{0,2,1:T(2,128)S(1)}, f32[512,16,2]{0,2,1:T(2,128)}, u32[]{:S(2)}) copy-start(f32[512,16,2]{0,2,1:T(2,128)} %param.20) | copy-start | bytes 196612
  25.4 14.3 %copy-start.7 = (f32[96,128]{1,0:T(8,128)S(1)}, f32[96,128]{1,0:T(8,128)}, u32[]{:S(2)}) copy-start(f32[96,128]{1,0:T(8,128)} %constant.14.clone.table_ref) | copy-start | bytes 147460
  40.7 12.0 %copy-start.4 = (f32[248,128]{1,0:T(8,128)S(1)}, f32[248,128]{1,0:T(8,128)}, u32[]{:S(2)}) copy-start(f32[248,128]{1,0:T(8,128)} %constant.13.clone.table_ref) | copy-start | bytes 380932
  52.7 12.6 %copy-start = (bf16[16,256,128]{2,1,0:T(8,128)(2,1)S(1)}, bf16[16,256,128]{2,1,0:T(8,128)(2,1)}, u32[]{:S(2)}) copy-start(bf16[16,256,128]{2,1,0:T(8,128)(2,1)} %proj_ref.1) | copy-start | bytes 3145732
  52.7 12.6 %copy-start.1 = (bf16[8,2,128,128]{3,2,1,0:T(8,128)(2,1)S(1)}, bf16[8,2,128,128]{3,2,1,0:T(8,128)(2,1)}, u32[]{:S(2)}) copy-start(bf16[8,2,128,128]{3,2,1,0:T(8,128)(2,1)} %blocks_ref.1) | copy-start | bytes 1572868
  53.3 12.0 %copy-start.6 = (f32[128,128]{1,0:T(8,128)S(1)}, f32[128,128]{1,0:T(8,128)}, u32[]{:S(2)}) copy-start(f32[128,128]{1,0:T(8,128)} %constant.11.clone.table_ref) | copy-start | bytes 196612

commit v6 on v5

--- a/solution.py
+++ b/solution.py
@@ -16,7 +16,7 @@
 NU = 12
 LINES = (96, 4, 128)
 ROWS = 384
-ORDER_X = (24, 27, 4, 12, 25, 10, 26, 19, 28, 1, 11, 6, 17, 14, 23, 16, 13, 20, 0, 5, 30, 8, 2, 21, 31, 29, 3, 22, 7, 15, 9, 18)
+ORDER_X = (11, 17, 7, 6, 3, 26, 22, 28, 13, 1, 29, 4, 15, 5, 21, 10, 12, 2, 20, 31, 18, 23, 16, 14, 25, 9, 30, 0, 8, 24, 19, 27)
 ORDER_Y = tuple(2 * z + x for x in range(2) for z in range(8))
 NV = 40
 CELLS = 512
@@ -226,8 +226,8 @@
             cells[128 * h + 8 * t : 128 * h + 8 * t + 8, pl.ds(lane, 256)] = wide
     phase_high = mm(tables_ref[256:384, 0:128], picks).astype(BF16)
     phase_low = mm(tables_ref[256:384, 128:256], picks).astype(BF16)
-    high, low = halves(cells[...])
-    out = mm(phase_high, high) + mm(phase_high, low) + mm(phase_low, high)
+    phase = jnp.concatenate([phase_high, phase_high, phase_low], axis=1)
+    out = mm(phase, thrice(cells[...], 0))
     out_ref[...] = out.astype(BF16)
 
 

time: 68.1 us -> 68.1 us (level)
  no operation moved by 1% of the time
where the time goes in v6:
time: 68.1 us; the launch traced here: 67.8 us
  blocking collectives  61 us (90%)
  Pallas kernels  6.62 us (10%)
    all_to_all x4, blocking collectives, swap(): lax.all_to_all(blocks, axis, 0, 0, axis_index_groups=[list(order)], tiled...  61 us
    pallas_call x1, Pallas kernels, body(): call(spread_kernel, [held(128, CELLS, dtype=BF16), held(32, SLOTS), held(...  2.46 us
    pallas_call x1, Pallas kernels, body(): call(gather_kernel, [shape(2, SOURCES)], [VM] * 6, [pltpu.SMEM((8, 128),...  1.99 us

profile of v6, /device:TPU:1, one launch (start us, length us, event | category | flops | bytes accessed | tf_op | source)
XLA Modules:
  0.0 67.8 jit_solution(12485469166585510206)
XLA Ops:
  0.0 2.5 %shard_map.127 = (bf16[128,512]{1,0:T(8,128)(2,1)S(1)}, f32[32,128]{1,0:T(8,128)S(1)}, s32[24,128]{1,0:T(8,128)S(1)}) custom-call(f32[2,1536]{1,0:T(2,128)} %charges_hbm.1, s32[12,128]{1,0:T(8,128)} %bitcast.23, s32[3,16]{1,0:T(4,128)} %bitcast.24, s32[2,8]{1,0:T(2,128)} %bitcast.25, bf16[16,256,128]{2,1,0:T(8,128)(2,1)} %proj_ref.1, ...), custom_call_target="tpu_custom_call" | custom-call | flops 1000000000 | bytes 2000000 | tf_op jit(solution)/shard_map/pallas_call | solution.py:474
  2.5 0.0 copy-start.5
  2.5 22.3 %all_to_all.20 = bf16[16,8,512]{2,1,0:T(8,128)(2,1)S(1)} all-to-all(bf16[16,8,512]{2,1,0:T(8,128)(2,1)S(1)} %bitcast.14), channel_id=1, replica_groups={{0,2,4,6,8,10,12,14,1,3,5,7,9,11,13,15},{16,18,20,22,24,26,28,30,17,19,..., dimensions={0} | all-to-all | bytes 262144 | tf_op jit(solution)/shard_map/all_to_all | solution.py:466
  24.8 0.0 copy-done.5
  24.8 0.6 shard_map.128
  25.3 0.0 copy-start.2
  25.4 0.0 copy-start.3
  25.4 0.0 copy-start.7
  25.4 14.7 %all_to_all.21 = bf16[32,3,4,128]{3,2,1,0:T(4,128)(2,1)S(1)} all-to-all(bf16[32,3,4,128]{3,2,1,0:T(4,128)(2,1)S(1)} %bitcast.17), channel_id=1, replica_groups={{176,272,112,96,48,416,352,448,208,16,464,64,240,80,336,160,192,32,320,..., dimensions={0} | all-to-all | bytes 196608 | tf_op jit(solution)/shard_map/all_to_all | solution.py:466
  40.1 0.0 copy-done.2
  40.1 0.0 copy-done.3
  40.1 0.0 copy-done.7
  40.1 1.0 %shard_map.129 = bf16[96,4,128]{2,1,0:T(4,128)(2,1)S(1)} custom-call(bf16[96,4,128]{2,1,0:T(4,128)(2,1)S(1)} %bitcast.18, f32[16,2,512]{2,1,0:T(2,128)S(1)} %bitcast.21, f32[16,2,512]{2,1,0:T(2,128)S(1)} %bitcast.22, f32[96,128]{1,0:T(8,128)S(1)} %copy-done.7), custom_call_target="tpu_custom_call" | custom-call | flops 1000000000 | bytes 1000000 | tf_op jit(solution)/shard_map/pallas_call | solution.py:504
  41.1 0.0 copy-start.4
  41.1 11.7 %all_to_all.22 = bf16[32,3,4,128]{3,2,1,0:T(4,128)(2,1)S(1)} all-to-all(bf16[32,3,4,128]{3,2,1,0:T(4,128)(2,1)S(1)} %bitcast.19), channel_id=1, replica_groups={{176,272,112,96,48,416,352,448,208,16,464,64,240,80,336,160,192,32,320,..., dimensions={0} | all-to-all | bytes 196608 | tf_op jit(solution)/shard_map/all_to_all | solution.py:466
  52.8 0.0 copy-done.4
  52.8 0.0 copy-start
  52.8 0.0 copy-start.1
  52.8 0.6 shard_map.130
  53.4 0.0 copy-start.6
  53.4 12.3 %all_to_all.23 = bf16[16,8,512]{2,1,0:T(8,128)(2,1)S(1)} all-to-all(bf16[16,8,512]{2,1,0:T(8,128)(2,1)S(1)} %bitcast.16), channel_id=1, replica_groups={{0,2,4,6,8,10,12,14,1,3,5,7,9,11,13,15},{16,18,20,22,24,26,28,30,17,19,..., dimensions={0} | all-to-all | bytes 262144 | tf_op jit(solution)/shard_map/all_to_all | solution.py:466
  65.8 0.0 copy-done
  65.8 0.0 copy-done.1
  65.8 0.0 copy-done.6
  65.8 2.0 %shard_map.131 = f32[2,1536]{1,0:T(2,128)} custom-call(bf16[128,512]{1,0:T(8,128)(2,1)S(1)} %bitcast.13, s32[24,128]{1,0:T(8,128)S(1)} %get-tuple-element.9.ints_ref, bf16[16,256,128]{2,1,0:T(8,128)(2,1)S(1)} %copy-done, f32[32,128]{1,0:T(8,128)S(1)} %get-tuple-element.10.slots_ref, bf16[8,2,128,128]{3,2,1,0:T(8,128)(2,1)S(1)} %copy-done.1, ...), custom_call_target="tpu_custom_call" | custom-call | flops 1000000000 | bytes 2000000 | tf_op jit(solution)/shard_map/pallas_call | solution.py:510
Async XLA Ops:
  2.5 22.3 %copy-start.5 = (f32[240,128]{1,0:T(8,128)S(1)}, f32[240,128]{1,0:T(8,128)}, u32[]{:S(2)}) copy-start(f32[240,128]{1,0:T(8,128)} %constant.12.clone.table_ref) | copy-start | bytes 368644
  25.3 14.7 %copy-start.2 = (f32[512,16,2]{0,2,1:T(2,128)S(1)}, f32[512,16,2]{0,2,1:T(2,128)}, u32[]{:S(2)}) copy-start(f32[512,16,2]{0,2,1:T(2,128)} %param.19) | copy-start | bytes 196612
  25.4 14.7 %copy-start.3 = (f32[512,16,2]{0,2,1:T(2,128)S(1)}, f32[512,16,2]{0,2,1:T(2,128)}, u32[]{:S(2)}) copy-start(f32[512,16,2]{0,2,1:T(2,128)} %param.20) | copy-start | bytes 196612
  25.4 14.7 %copy-start.7 = (f32[96,128]{1,0:T(8,128)S(1)}, f32[96,128]{1,0:T(8,128)}, u32[]{:S(2)}) copy-start(f32[96,128]{1,0:T(8,128)} %constant.14.clone.table_ref) | copy-start | bytes 147460
  41.1 11.7 %copy-start.4 = (f32[248,128]{1,0:T(8,128)S(1)}, f32[248,128]{1,0:T(8,128)}, u32[]{:S(2)}) copy-start(f32[248,128]{1,0:T(8,128)} %constant.13.clone.table_ref) | copy-start | bytes 380932
  52.8 13.0 %copy-start = (bf16[16,256,128]{2,1,0:T(8,128)(2,1)S(1)}, bf16[16,256,128]{2,1,0:T(8,128)(2,1)}, u32[]{:S(2)}) copy-start(bf16[16,256,128]{2,1,0:T(8,128)(2,1)} %proj_ref.1) | copy-start | bytes 3145732
  52.8 13.0 %copy-start.1 = (bf16[8,2,128,128]{3,2,1,0:T(8,128)(2,1)S(1)}, bf16[8,2,128,128]{3,2,1,0:T(8,128)(2,1)}, u32[]{:S(2)}) copy-start(bf16[8,2,128,128]{3,2,1,0:T(8,128)(2,1)} %blocks_ref.1) | copy-start | bytes 1572868
  53.4 12.3 %copy-start.6 = (f32[128,128]{1,0:T(8,128)S(1)}, f32[128,128]{1,0:T(8,128)}, u32[]{:S(2)}) copy-start(f32[128,128]{1,0:T(8,128)} %constant.11.clone.table_ref) | copy-start | bytes 196612

commit v7 on v6

--- a/solution.py
+++ b/solution.py
@@ -16,7 +16,7 @@
 NU = 12
 LINES = (96, 4, 128)
 ROWS = 384
-ORDER_X = (11, 17, 7, 6, 3, 26, 22, 28, 13, 1, 29, 4, 15, 5, 21, 10, 12, 2, 20, 31, 18, 23, 16, 14, 25, 9, 30, 0, 8, 24, 19, 27)
+ORDER_X = (24, 27, 4, 12, 25, 10, 26, 19, 28, 1, 11, 6, 17, 14, 23, 16, 13, 20, 0, 5, 30, 8, 2, 21, 31, 29, 3, 22, 7, 15, 9, 18)
 ORDER_Y = tuple(2 * z + x for x in range(2) for z in range(8))
 NV = 40
 CELLS = 512

time: 68.1 us -> 68.1 us (level)
  no operation moved by 1% of the time
where the time goes in v7:
time: 68.1 us; the launch traced here: 67.3 us
  blocking collectives  60.5 us (89%)
  Pallas kernels  6.62 us (10%)
    all_to_all x4, blocking collectives, swap(): lax.all_to_all(blocks, axis, 0, 0, axis_index_groups=[list(order)], tiled...  60.5 us
    pallas_call x1, Pallas kernels, body(): call(spread_kernel, [held(128, CELLS, dtype=BF16), held(32, SLOTS), held(...  2.46 us
    pallas_call x1, Pallas kernels, body(): call(gather_kernel, [shape(2, SOURCES)], [VM] * 6, [pltpu.SMEM((8, 128),...  1.99 us

profile of v7, /device:TPU:1, one launch (start us, length us, event | category | flops | bytes accessed | tf_op | source)
XLA Modules:
  0.0 67.3 jit_solution(17445361659995742030)
XLA Ops:
  0.0 2.5 %shard_map.127 = (bf16[128,512]{1,0:T(8,128)(2,1)S(1)}, f32[32,128]{1,0:T(8,128)S(1)}, s32[24,128]{1,0:T(8,128)S(1)}) custom-call(f32[2,1536]{1,0:T(2,128)} %charges_hbm.1, s32[12,128]{1,0:T(8,128)} %bitcast.23, s32[3,16]{1,0:T(4,128)} %bitcast.24, s32[2,8]{1,0:T(2,128)} %bitcast.25, bf16[16,256,128]{2,1,0:T(8,128)(2,1)} %proj_ref.1, ...), custom_call_target="tpu_custom_call" | custom-call | flops 1000000000 | bytes 2000000 | tf_op jit(solution)/shard_map/pallas_call | solution.py:474
  2.5 0.0 copy-start.5
  2.5 22.3 %all_to_all.20 = bf16[16,8,512]{2,1,0:T(8,128)(2,1)S(1)} all-to-all(bf16[16,8,512]{2,1,0:T(8,128)(2,1)S(1)} %bitcast.14), channel_id=1, replica_groups={{0,2,4,6,8,10,12,14,1,3,5,7,9,11,13,15},{16,18,20,22,24,26,28,30,17,19,..., dimensions={0} | all-to-all | bytes 262144 | tf_op jit(solution)/shard_map/all_to_all | solution.py:466
  24.8 0.0 copy-done.5
  24.8 0.6 shard_map.128
  25.3 0.0 copy-start.2
  25.4 0.0 copy-start.3
  25.4 0.0 copy-start.7
  25.4 14.3 %all_to_all.21 = bf16[32,3,4,128]{3,2,1,0:T(4,128)(2,1)S(1)} all-to-all(bf16[32,3,4,128]{3,2,1,0:T(4,128)(2,1)S(1)} %bitcast.17), channel_id=1, replica_groups={{384,432,64,192,400,160,416,304,448,16,176,96,272,224,368,256,208,320,0..., dimensions={0} | all-to-all | bytes 196608 | tf_op jit(solution)/shard_map/all_to_all | solution.py:466
  39.6 0.0 copy-done.2
  39.6 0.0 copy-done.3
  39.6 0.0 copy-done.7
  39.6 1.0 %shard_map.129 = bf16[96,4,128]{2,1,0:T(4,128)(2,1)S(1)} custom-call(bf16[96,4,128]{2,1,0:T(4,128)(2,1)S(1)} %bitcast.18, f32[16,2,512]{2,1,0:T(2,128)S(1)} %bitcast.21, f32[16,2,512]{2,1,0:T(2,128)S(1)} %bitcast.22, f32[96,128]{1,0:T(8,128)S(1)} %copy-done.7), custom_call_target="tpu_custom_call" | custom-call | flops 1000000000 | bytes 1000000 | tf_op jit(solution)/shard_map/pallas_call | solution.py:504
  40.6 0.0 copy-start.4
  40.7 12.0 %all_to_all.22 = bf16[32,3,4,128]{3,2,1,0:T(4,128)(2,1)S(1)} all-to-all(bf16[32,3,4,128]{3,2,1,0:T(4,128)(2,1)S(1)} %bitcast.19), channel_id=1, replica_groups={{384,432,64,192,400,160,416,304,448,16,176,96,272,224,368,256,208,320,0..., dimensions={0} | all-to-all | bytes 196608 | tf_op jit(solution)/shard_map/all_to_all | solution.py:466
  52.6 0.0 copy-done.4
  52.7 0.0 copy-start
  52.7 0.0 copy-start.1
  52.7 0.6 shard_map.130
  53.3 0.0 copy-start.6
  53.3 12.0 %all_to_all.23 = bf16[16,8,512]{2,1,0:T(8,128)(2,1)S(1)} all-to-all(bf16[16,8,512]{2,1,0:T(8,128)(2,1)S(1)} %bitcast.16), channel_id=1, replica_groups={{0,2,4,6,8,10,12,14,1,3,5,7,9,11,13,15},{16,18,20,22,24,26,28,30,17,19,..., dimensions={0} | all-to-all | bytes 262144 | tf_op jit(solution)/shard_map/all_to_all | solution.py:466
  65.3 0.0 copy-done
  65.3 0.0 copy-done.1
  65.3 0.0 copy-done.6
  65.3 2.0 %shard_map.131 = f32[2,1536]{1,0:T(2,128)} custom-call(bf16[128,512]{1,0:T(8,128)(2,1)S(1)} %bitcast.13, s32[24,128]{1,0:T(8,128)S(1)} %get-tuple-element.9.ints_ref, bf16[16,256,128]{2,1,0:T(8,128)(2,1)S(1)} %copy-done, f32[32,128]{1,0:T(8,128)S(1)} %get-tuple-element.10.slots_ref, bf16[8,2,128,128]{3,2,1,0:T(8,128)(2,1)S(1)} %copy-done.1, ...), custom_call_target="tpu_custom_call" | custom-call | flops 1000000000 | bytes 2000000 | tf_op jit(solution)/shard_map/pallas_call | solution.py:510
Async XLA Ops:
  2.5 22.3 %copy-start.5 = (f32[240,128]{1,0:T(8,128)S(1)}, f32[240,128]{1,0:T(8,128)}, u32[]{:S(2)}) copy-start(f32[240,128]{1,0:T(8,128)} %constant.12.clone.table_ref) | copy-start | bytes 368644
  25.3 14.3 %copy-start.2 = (f32[512,16,2]{0,2,1:T(2,128)S(1)}, f32[512,16,2]{0,2,1:T(2,128)}, u32[]{:S(2)}) copy-start(f32[512,16,2]{0,2,1:T(2,128)} %param.19) | copy-start | bytes 196612
  25.4 14.3 %copy-start.3 = (f32[512,16,2]{0,2,1:T(2,128)S(1)}, f32[512,16,2]{0,2,1:T(2,128)}, u32[]{:S(2)}) copy-start(f32[512,16,2]{0,2,1:T(2,128)} %param.20) | copy-start | bytes 196612
  25.4 14.3 %copy-start.7 = (f32[96,128]{1,0:T(8,128)S(1)}, f32[96,128]{1,0:T(8,128)}, u32[]{:S(2)}) copy-start(f32[96,128]{1,0:T(8,128)} %constant.14.clone.table_ref) | copy-start | bytes 147460
  40.6 12.0 %copy-start.4 = (f32[248,128]{1,0:T(8,128)S(1)}, f32[248,128]{1,0:T(8,128)}, u32[]{:S(2)}) copy-start(f32[248,128]{1,0:T(8,128)} %constant.13.clone.table_ref) | copy-start | bytes 380932
  52.7 12.6 %copy-start = (bf16[16,256,128]{2,1,0:T(8,128)(2,1)S(1)}, bf16[16,256,128]{2,1,0:T(8,128)(2,1)}, u32[]{:S(2)}) copy-start(bf16[16,256,128]{2,1,0:T(8,128)(2,1)} %proj_ref.1) | copy-start | bytes 3145732
  52.7 12.6 %copy-start.1 = (bf16[8,2,128,128]{3,2,1,0:T(8,128)(2,1)S(1)}, bf16[8,2,128,128]{3,2,1,0:T(8,128)(2,1)}, u32[]{:S(2)}) copy-start(bf16[8,2,128,128]{3,2,1,0:T(8,128)(2,1)} %blocks_ref.1) | copy-start | bytes 1572868
  53.3 12.0 %copy-start.6 = (f32[128,128]{1,0:T(8,128)S(1)}, f32[128,128]{1,0:T(8,128)}, u32[]{:S(2)}) copy-start(f32[128,128]{1,0:T(8,128)} %constant.11.clone.table_ref) | copy-start | bytes 196612
